TPU v7x, 32 devices: a whole 2x2x4 slice. The times are simulated.
32 devices in a mesh: dp: 16 (over z, y, core), tensor: 2 (over x).
Axes of the slice: x: 2, y: 2, z: 4, core: 2. Of those that a mesh axis runs over, the one named last changes fastest.
Arguments:
- char_ids: int32 [8192, 50], P(('dp', 'tensor')), may hold values from 0 to 261
- mask_pos: int32 [16, 76], P('dp'), may hold values from 0 to 511
- out_grad: float32 [16, 76, 768], P('dp'), may hold values from -6 to 6
- char_table: bfloat16 [262, 16], replicated, may hold values from -6 to 6
- conv_weight: bfloat16 [112, 2048], P(None, ('dp', 'tensor')), may hold values from -1.5 to 1.5
- conv_bias: bfloat16 [2048], P(('dp', 'tensor')), may hold values from -8 to -2
- highway_weight: bfloat16 [2, 2048, 2, 2048], P(None, None, None, ('dp', 'tensor')), may hold values from -0.125 to 0.125
- highway_bias: bfloat16 [2, 2, 2048], P(None, None, ('dp', 'tensor')), may hold values from -3 to 3
- proj_weight: bfloat16 [2048, 768], P(('dp', 'tensor')), may hold values from -0.0625 to 0.0625
- proj_bias: bfloat16 [768], replicated, may hold values from -2 to 2
- qkv_weight: bfloat16 [768, 3, 768], P(None, None, 'tensor'), may hold values from -0.21875 to 0.21875
- qv_bias: bfloat16 [2, 768], P(None, 'tensor'), may hold values from -2 to 2
- out_weight: bfloat16 [768, 768], P('tensor'), may hold values from -3 to 3
- out_bias: bfloat16 [768], replicated, may hold values from -2 to 2
- ln1_gain: bfloat16 [768], replicated, may hold values from 0.25 to 1.75
- ln1_bias: bfloat16 [768], replicated, may hold values from -2 to 2
- up_weight: bfloat16 [768, 3072], P(None, 'tensor'), may hold values from -0.21875 to 0.21875
- up_bias: bfloat16 [3072], P('tensor'), may hold values from -2 to 2
- down_weight: bfloat16 [3072, 768], P('tensor'), may hold values from -0.109375 to 0.109375
- down_bias: bfloat16 [768], replicated, may hold values from -2 to 2
- ln2_gain: bfloat16 [768], replicated, may hold values from 0.25 to 1.75
- ln2_bias: bfloat16 [768], replicated, may hold values from -2 to 2
Outputs:
- layer_output: bfloat16 [8192, 768], P(('dp', 'tensor'))
- char_table_grad: float32 [262, 16], replicated
- conv_weight_grad: float32 [112, 2048], P(None, ('dp', 'tensor'))
- conv_bias_grad: float32 [2048], P(('dp', 'tensor'))
- highway_weight_grad: float32 [2, 2048, 2, 2048], P(None, None, None, ('dp', 'tensor'))
- highway_bias_grad: float32 [2, 2, 2048], P(None, None, ('dp', 'tensor'))
- proj_weight_grad: float32 [2048, 768], P(('dp', 'tensor'))
- proj_bias_grad: float32 [768], replicated
- qkv_weight_grad: float32 [768, 3, 768], P('dp', None, 'tensor')
- qv_bias_grad: float32 [2, 768], P(None, 'tensor')
- out_weight_grad: float32 [768, 768], P('tensor', 'dp')
- out_bias_grad: float32 [768], replicated
- ln1_gain_grad: float32 [768], replicated
- ln1_bias_grad: float32 [768], replicated
- up_weight_grad: float32 [768, 3072], P('dp', 'tensor')
- up_bias_grad: float32 [3072], P('tensor')
- down_weight_grad: float32 [3072, 768], P('tensor', 'dp')
- down_bias_grad: float32 [768], replicated
- ln2_gain_grad: float32 [768], replicated
- ln2_bias_grad: float32 [768], replicated
Inputs may be any that keep to these rules, and one draw needn't show every extreme that they name: `mask_pos`: positions within a sequence; a position may occur twice, its gradients then add. `char_ids`: every character slot of every word holds an id.
All inputs are finite; a program needn't handle non-finite values.
Results may differ from a plain program's by a relative error of at most 0.02.
Values may be sent and summed in bfloat16 or wider, within the bound.
A program may use at most 320 MiB of HBM per device.

v0:
```python
import math

import jax
import jax.numpy as jnp
from jax import lax
from jax.sharding import PartitionSpec as P

HEAD_DIM = 64
FILTERS = 2048
CHAR_DIM = 16
CHARS = 50
MAX_WIDTH = 7
HIGHWAYS = 2
LEN = 512
D = 768


channel_shares = (1, 2, 4, 8, 16, 32)
norm_eps = 1e-05
big_negative = -1e30


def exact_gelu(inputs):
    return jax.nn.gelu(inputs, approximate=False)


def gelu_slope(inputs):
    return jax.vjp(exact_gelu, inputs)[1](jnp.ones_like(inputs))[0]


def channel_masks():
    channel = jnp.arange(FILTERS, dtype=jnp.int32)
    bounds = jnp.array([portion * (FILTERS // 64) for portion in channel_shares], dtype=jnp.int32)
    filter_width = 1 + jnp.sum((channel[:, None] >= bounds[None, :]).astype(jnp.int32), axis=1)
    row_shift = jnp.arange(MAX_WIDTH * CHAR_DIM, dtype=jnp.int32) // CHAR_DIM
    weight_mask = (row_shift[:, None] < filter_width[None, :]).astype(jnp.float32)
    positions = jnp.arange(CHARS, dtype=jnp.int32)
    place_mask = positions[:, None] + filter_width[None, :] <= CHARS
    return (weight_mask, place_mask)


def char_windows(vectors):
    padded = jnp.pad(vectors, ((0, 0), (0, MAX_WIDTH - 1), (0, 0)))
    return jnp.concatenate(
        [padded[:, offset : offset + CHARS, :] for offset in range(MAX_WIDTH)], axis=2
    )


def conv_pool(word_chars, char_table, conv_masked, conv_full_bias, place_mask):
    onehot = (
        word_chars[:, :, None] == jnp.arange(char_table.shape[0], dtype=jnp.int32)[None, None, :]
    ).astype(jnp.bfloat16)
    char_vectors = jnp.einsum(
        "wcn,nd->wcd", onehot, char_table, preferred_element_type=jnp.float32
    ).astype(jnp.bfloat16)
    windows = char_windows(char_vectors)
    conv_out = jnp.einsum(
        "wcr,rf->wcf", windows, conv_masked, preferred_element_type=jnp.float32
    ) + conv_full_bias.astype(jnp.float32)
    masked = jnp.where(place_mask[None], conv_out, big_negative)
    row_max = jnp.max(masked, axis=1, keepdims=True)
    exp_terms = jnp.exp(masked - row_max)
    exp_total = jnp.sum(exp_terms, axis=1, keepdims=True)
    pooled = (row_max + jnp.log(exp_total))[:, 0, :]
    return (pooled, exp_terms / exp_total, onehot, windows)


def highway_forward(pooled, highway_full, highway_full_bias):
    highway_state = exact_gelu(pooled)
    kept_layers = []
    for layer_index in range(highway_full.shape[0]):
        state_low = highway_state.astype(jnp.bfloat16)
        pre_act = jnp.dot(
            state_low, highway_full[layer_index], preferred_element_type=jnp.float32
        ) + highway_full_bias[layer_index].astype(jnp.float32)
        half_width = pre_act.shape[1] // 2
        gate_open = jax.nn.sigmoid(pre_act[:, half_width:])
        kept_layers.append((highway_state, state_low, pre_act))
        highway_state = gate_open * highway_state + (1.0 - gate_open) * exact_gelu(
            pre_act[:, :half_width]
        )
    return (highway_state, kept_layers)


def highway_backward(grad_state, kept_layers, highway_full):
    weight_grads = []
    bias_grads = []
    for layer_index in reversed(range(len(kept_layers))):
        state_in, state_low, pre_act = kept_layers[layer_index]
        half_width = pre_act.shape[1] // 2
        nonlinear = pre_act[:, :half_width]
        gate_open = jax.nn.sigmoid(pre_act[:, half_width:])
        grad_gate = grad_state * (state_in - exact_gelu(nonlinear)) * gate_open * (1.0 - gate_open)
        grad_nonlinear = grad_state * (1.0 - gate_open) * gelu_slope(nonlinear)
        grad_pre = jnp.concatenate([grad_nonlinear, grad_gate], axis=1).astype(jnp.bfloat16)
        weight_grads.insert(
            0, jnp.einsum("rf,rg->fg", state_low, grad_pre, preferred_element_type=jnp.float32)
        )
        bias_grads.insert(0, jnp.sum(grad_pre, axis=0, dtype=jnp.float32))
        grad_state = grad_state * gate_open + jnp.einsum(
            "rg,fg->rf", grad_pre, highway_full[layer_index], preferred_element_type=jnp.float32
        )
    return (grad_state, jnp.stack(weight_grads), jnp.stack(bias_grads))


def norm_forward(summed, gain_vec, bias_vec):
    row_mean = jnp.mean(summed, axis=-1, keepdims=True)
    centred = summed - row_mean
    variance = jnp.mean(centred * centred, axis=-1, keepdims=True)
    inv_std = lax.rsqrt(variance + norm_eps)
    normalized = centred * inv_std
    return (normalized * gain_vec + bias_vec, normalized, inv_std)


def norm_backward(grad_out, normalized, inv_std, gain_vec):
    grad_norm = grad_out * gain_vec
    grad_in = inv_std * (
        grad_norm
        - jnp.mean(grad_norm, axis=-1, keepdims=True)
        - normalized * jnp.mean(grad_norm * normalized, axis=-1, keepdims=True)
    )
    return (grad_in, jnp.sum(grad_out * normalized, axis=0), jnp.sum(grad_out, axis=0))


def per_device(
    char_ids,
    mask_pos,
    out_grad,
    char_table,
    conv_weight,
    conv_bias,
    highway_weight,
    highway_bias,
    proj_weight,
    proj_bias,
    qkv_weight,
    qv_bias,
    out_weight,
    out_bias,
    ln1_gain,
    ln1_bias,
    up_weight,
    up_bias,
    down_weight,
    down_bias,
    ln2_gain,
    ln2_bias,
):
    tensor_index = lax.axis_index("tensor")
    conv_full, conv_full_bias, highway_gathered, highway_bias_gathered, proj_full = (
        lax.all_gather(conv_weight, ("dp", "tensor"), axis=1, tiled=True),
        lax.all_gather(conv_bias, ("dp", "tensor"), axis=0, tiled=True),
        lax.all_gather(highway_weight, ("dp", "tensor"), axis=3, tiled=True),
        lax.all_gather(highway_bias, ("dp", "tensor"), axis=2, tiled=True),
        lax.all_gather(proj_weight, ("dp", "tensor"), axis=0, tiled=True),
    )
    weight_mask, place_mask = channel_masks()
    conv_masked = conv_full * weight_mask.astype(jnp.bfloat16)
    row_count = char_ids.shape[0]
    block_rows = math.gcd(row_count, 64)
    block_count = row_count // block_rows
    word_blocks = char_ids.reshape(block_count, block_rows, CHARS)

    def pool_block(word_block):
        return conv_pool(word_block, char_table, conv_masked, conv_full_bias, place_mask)[0]

    pooled = lax.map(pool_block, word_blocks).reshape(row_count, FILTERS)
    highway_full = highway_gathered.reshape(HIGHWAYS, FILTERS, 2 * FILTERS)
    highway_full_bias = highway_bias_gathered.reshape(HIGHWAYS, 2 * FILTERS)
    highway_state, kept_layers = highway_forward(pooled, highway_full, highway_full_bias)
    state_low = highway_state.astype(jnp.bfloat16)
    embedded = jnp.dot(state_low, proj_full, preferred_element_type=jnp.float32) + proj_bias.astype(
        jnp.float32
    )
    gathered = lax.all_gather(embedded.astype(jnp.bfloat16), "tensor", axis=0, tiled=True)
    group_rows = gathered.shape[0]
    seq_count = group_rows // LEN
    local_width = qkv_weight.shape[2]
    heads_here = local_width // HEAD_DIM
    qkv_flat = qkv_weight.reshape(D, 3 * local_width)
    qkv_bias = jnp.stack([qv_bias[0], jnp.zeros_like(qv_bias[0]), qv_bias[1]]).astype(jnp.float32)
    projected = (
        jnp.dot(gathered, qkv_flat, preferred_element_type=jnp.float32).reshape(
            group_rows, 3, local_width
        )
        + qkv_bias[None]
    ).astype(jnp.bfloat16)

    def head_view(source, component):
        return source[:, component].reshape(seq_count, LEN, heads_here, HEAD_DIM)

    query_low = head_view(projected, 0)
    keys_low = head_view(projected, 1)
    values_low = head_view(projected, 2)
    score_scale = 1.0 / math.sqrt(HEAD_DIM)
    scores = (
        jnp.einsum("bqhd,bkhd->bhqk", query_low, keys_low, preferred_element_type=jnp.float32)
        * score_scale
    )
    row_max = jnp.max(scores, axis=-1, keepdims=True)
    exp_terms = jnp.exp(scores - row_max)
    exp_total = jnp.sum(exp_terms, axis=-1, keepdims=True)
    log_totals = row_max + jnp.log(exp_total)
    attn_probs = exp_terms / exp_total
    mixed_low = (
        jnp.einsum(
            "bhqk,bkhd->bqhd",
            attn_probs.astype(jnp.bfloat16),
            values_low,
            preferred_element_type=jnp.float32,
        )
        .reshape(group_rows, local_width)
        .astype(jnp.bfloat16)
    )
    attended = lax.psum_scatter(
        jnp.dot(mixed_low, out_weight, preferred_element_type=jnp.float32).astype(jnp.bfloat16),
        "tensor",
        scatter_dimension=0,
        tiled=True,
    ).astype(jnp.float32)
    gain_one = ln1_gain.astype(jnp.float32)
    gain_two = ln2_gain.astype(jnp.float32)
    normed, normalized_one, inv_std_one = norm_forward(
        embedded + attended + out_bias.astype(jnp.float32), gain_one, ln1_bias.astype(jnp.float32)
    )
    ffn_in = lax.all_gather(normed.astype(jnp.bfloat16), "tensor", axis=0, tiled=True)
    hidden_pre = jnp.dot(ffn_in, up_weight, preferred_element_type=jnp.float32) + up_bias.astype(
        jnp.float32
    )
    hidden_low = exact_gelu(hidden_pre).astype(jnp.bfloat16)
    ffn_out = lax.psum_scatter(
        jnp.dot(hidden_low, down_weight, preferred_element_type=jnp.float32).astype(jnp.bfloat16),
        "tensor",
        scatter_dimension=0,
        tiled=True,
    ).astype(jnp.float32)
    result, normalized_two, inv_std_two = norm_forward(
        normed + ffn_out + down_bias.astype(jnp.float32), gain_two, ln2_bias.astype(jnp.float32)
    )
    local_rows = (
        jnp.arange(seq_count, dtype=jnp.int32)[:, None] * LEN + mask_pos - tensor_index * row_count
    )
    valid_rows = (local_rows >= 0) & (local_rows < row_count)
    target_rows = jnp.where(valid_rows, local_rows, row_count).reshape(-1)
    grad_final = (
        jnp.zeros((row_count, D), jnp.float32)
        .at[target_rows]
        .add(out_grad.reshape(-1, D), mode="drop")
    )
    grad_second, ln2_gain_grad, ln2_bias_grad = norm_backward(
        grad_final, normalized_two, inv_std_two, gain_two
    )
    ffn_grad_low = grad_second.astype(jnp.bfloat16)
    down_bias_grad = jnp.sum(ffn_grad_low, axis=0, dtype=jnp.float32)
    ffn_grad = lax.all_gather(ffn_grad_low, "tensor", axis=0, tiled=True)
    down_weight_grad = jnp.einsum(
        "rf,rd->fd", hidden_low, ffn_grad, preferred_element_type=jnp.float32
    )
    grad_hidden = jnp.einsum("rd,fd->rf", ffn_grad, down_weight, preferred_element_type=jnp.float32)
    grad_pre_low = (grad_hidden * gelu_slope(hidden_pre)).astype(jnp.bfloat16)
    up_bias_grad = jnp.sum(grad_pre_low, axis=0, dtype=jnp.float32)
    up_weight_grad = jnp.einsum(
        "rd,rf->df", ffn_in, grad_pre_low, preferred_element_type=jnp.float32
    )
    grad_normed = grad_second + lax.psum_scatter(
        jnp.einsum("rf,df->rd", grad_pre_low, up_weight, preferred_element_type=jnp.float32).astype(
            jnp.bfloat16
        ),
        "tensor",
        scatter_dimension=0,
        tiled=True,
    ).astype(jnp.float32)
    grad_first, ln1_gain_grad, ln1_bias_grad = norm_backward(
        grad_normed, normalized_one, inv_std_one, gain_one
    )
    attn_grad_low = grad_first.astype(jnp.bfloat16)
    out_bias_grad = jnp.sum(attn_grad_low, axis=0, dtype=jnp.float32)
    attn_grad = lax.all_gather(attn_grad_low, "tensor", axis=0, tiled=True)
    out_weight_grad = jnp.einsum(
        "rw,rd->wd", mixed_low, attn_grad, preferred_element_type=jnp.float32
    )
    grad_mixed = (
        jnp.einsum("rd,wd->rw", attn_grad, out_weight, preferred_element_type=jnp.float32)
        .astype(jnp.bfloat16)
        .reshape(seq_count, LEN, heads_here, HEAD_DIM)
    )
    scores_again = (
        jnp.einsum("bqhd,bkhd->bhqk", query_low, keys_low, preferred_element_type=jnp.float32)
        * score_scale
    )
    probs_again = jnp.exp(scores_again - log_totals)
    grad_values = jnp.einsum(
        "bhqk,bqhd->bkhd",
        probs_again.astype(jnp.bfloat16),
        grad_mixed,
        preferred_element_type=jnp.float32,
    )
    grad_probs = jnp.einsum(
        "bqhd,bkhd->bhqk", grad_mixed, values_low, preferred_element_type=jnp.float32
    )
    grad_scores = (
        probs_again * (grad_probs - jnp.sum(probs_again * grad_probs, axis=-1, keepdims=True))
    ).astype(jnp.bfloat16)
    grad_query = (
        jnp.einsum("bhqk,bkhd->bqhd", grad_scores, keys_low, preferred_element_type=jnp.float32)
        * score_scale
    )
    grad_keys = (
        jnp.einsum("bhqk,bqhd->bkhd", grad_scores, query_low, preferred_element_type=jnp.float32)
        * score_scale
    )
    grad_projected = jnp.stack(
        [
            grad_query.reshape(group_rows, local_width),
            grad_keys.reshape(group_rows, local_width),
            grad_values.reshape(group_rows, local_width),
        ],
        axis=1,
    ).astype(jnp.bfloat16)
    projected_sums = jnp.sum(grad_projected, axis=0, dtype=jnp.float32)
    qv_bias_grad = jnp.stack([projected_sums[0], projected_sums[2]])
    grad_flat = grad_projected.reshape(group_rows, 3 * local_width)
    qkv_weight_grad = jnp.einsum(
        "rd,rw->dw", gathered, grad_flat, preferred_element_type=jnp.float32
    ).reshape(D, 3, local_width)
    grad_embedded = grad_first + lax.psum_scatter(
        jnp.einsum("rw,dw->rd", grad_flat, qkv_flat, preferred_element_type=jnp.float32).astype(
            jnp.bfloat16
        ),
        "tensor",
        scatter_dimension=0,
        tiled=True,
    ).astype(jnp.float32)
    qkv_weight_grad, out_weight_grad, up_weight_grad, down_weight_grad = (
        lax.psum_scatter(qkv_weight_grad, "dp", scatter_dimension=0, tiled=True),
        lax.psum_scatter(out_weight_grad, "dp", scatter_dimension=1, tiled=True),
        lax.psum_scatter(up_weight_grad, "dp", scatter_dimension=0, tiled=True),
        lax.psum_scatter(down_weight_grad, "dp", scatter_dimension=1, tiled=True),
    )
    qv_bias_grad, up_bias_grad = lax.psum((qv_bias_grad, up_bias_grad), "dp")
    embedded_grad_low = grad_embedded.astype(jnp.bfloat16)
    proj_bias_grad = jnp.sum(embedded_grad_low, axis=0, dtype=jnp.float32)
    proj_grad = jnp.einsum(
        "rf,rd->fd", state_low, embedded_grad_low, preferred_element_type=jnp.float32
    )
    grad_state = jnp.einsum(
        "rd,fd->rf", embedded_grad_low, proj_full, preferred_element_type=jnp.float32
    )
    grad_state, highway_flat_grad, highway_flat_bias_grad = highway_backward(
        grad_state, kept_layers, highway_full
    )
    highway_grad = highway_flat_grad.reshape(HIGHWAYS, FILTERS, 2, FILTERS)
    highway_bias_grad = highway_flat_bias_grad.reshape(HIGHWAYS, 2, FILTERS)
    pooled_grad = grad_state * gelu_slope(pooled)
    char_dim = char_table.shape[1]

    def conv_step(running, block_inputs):
        word_block, block_grad = block_inputs
        unused_pooled, pool_weights, onehot, windows = conv_pool(
            word_block, char_table, conv_masked, conv_full_bias, place_mask
        )
        grad_conv = (pool_weights * block_grad[:, None, :]).astype(jnp.bfloat16)
        weight_total = running[0] + jnp.einsum(
            "wcr,wcf->rf", windows, grad_conv, preferred_element_type=jnp.float32
        )
        bias_total = running[1] + jnp.sum(grad_conv, axis=(0, 1), dtype=jnp.float32)
        grad_windows = jnp.einsum(
            "wcf,rf->wcr", grad_conv, conv_masked, preferred_element_type=jnp.float32
        )
        grad_vectors = sum(
            (
                jnp.pad(
                    grad_windows[:, :, offset * char_dim : (offset + 1) * char_dim],
                    ((0, 0), (offset, MAX_WIDTH - 1 - offset), (0, 0)),
                )
                for offset in range(MAX_WIDTH)
            )
        )[:, :CHARS, :]
        table_total = running[2] + jnp.einsum(
            "wcn,wcd->nd",
            onehot,
            grad_vectors.astype(jnp.bfloat16),
            preferred_element_type=jnp.float32,
        )
        return ((weight_total, bias_total, table_total), None)

    start_totals = (
        jnp.zeros(conv_full.shape, jnp.float32),
        jnp.zeros((FILTERS,), jnp.float32),
        jnp.zeros(char_table.shape, jnp.float32),
    )
    conv_totals, unused_rest = lax.scan(
        conv_step,
        start_totals,
        (word_blocks, pooled_grad.reshape(block_count, block_rows, FILTERS)),
    )
    conv_weight_total = conv_totals[0] * weight_mask
    conv_part, conv_bias_part, highway_part, highway_bias_part, proj_part = (
        lax.psum_scatter(conv_weight_total, ("dp", "tensor"), scatter_dimension=1, tiled=True),
        lax.psum_scatter(conv_totals[1], ("dp", "tensor"), scatter_dimension=0, tiled=True),
        lax.psum_scatter(highway_grad, ("dp", "tensor"), scatter_dimension=3, tiled=True),
        lax.psum_scatter(highway_bias_grad, ("dp", "tensor"), scatter_dimension=2, tiled=True),
        lax.psum_scatter(proj_grad, ("dp", "tensor"), scatter_dimension=0, tiled=True),
    )
    (
        table_grad,
        proj_bias_grad,
        out_bias_grad,
        ln1_gain_grad,
        ln1_bias_grad,
        down_bias_grad,
        ln2_gain_grad,
        ln2_bias_grad,
    ) = lax.psum(
        (
            conv_totals[2],
            proj_bias_grad,
            out_bias_grad,
            ln1_gain_grad,
            ln1_bias_grad,
            down_bias_grad,
            ln2_gain_grad,
            ln2_bias_grad,
        ),
        ("dp", "tensor"),
    )
    return (
        result.astype(jnp.bfloat16),
        table_grad,
        conv_part,
        conv_bias_part,
        highway_part,
        highway_bias_part,
        proj_part,
        proj_bias_grad,
        qkv_weight_grad,
        qv_bias_grad,
        out_weight_grad,
        out_bias_grad,
        ln1_gain_grad,
        ln1_bias_grad,
        up_weight_grad,
        up_bias_grad,
        down_weight_grad,
        down_bias_grad,
        ln2_gain_grad,
        ln2_bias_grad,
    )


def solution(mesh):
    placed = (
        P(("dp", "tensor"), None),
        P("dp", None),
        P("dp", None, None),
        P(),
        P(None, ("dp", "tensor")),
        P(("dp", "tensor")),
        P(None, None, None, ("dp", "tensor")),
        P(None, None, ("dp", "tensor")),
        P(("dp", "tensor"), None),
        P(),
        P(None, None, "tensor"),
        P(None, "tensor"),
        P("tensor", None),
        P(),
        P(),
        P(),
        P(None, "tensor"),
        P("tensor"),
        P("tensor", None),
        P(),
        P(),
        P(),
    )
    return jax.shard_map(
        per_device,
        mesh=mesh,
        in_specs=placed,
        out_specs=(
            P(("dp", "tensor"), None),
            P(),
            P(None, ("dp", "tensor")),
            P(("dp", "tensor")),
            P(None, None, None, ("dp", "tensor")),
            P(None, None, ("dp", "tensor")),
            P(("dp", "tensor"), None),
            P(),
            P("dp", None, "tensor"),
            P(None, "tensor"),
            P("tensor", "dp"),
            P(),
            P(),
            P(),
            P("dp", "tensor"),
            P("tensor"),
            P("tensor", "dp"),
            P(),
            P(),
            P(),
        ),
        check_vma=False,
    )
```

profile of v0, /device:TPU:0, one launch (start us, length us, event | category | flops | bytes accessed | tf_op | source)
XLA Modules:
  0.0 2340.7 jit_solution(4757709195045941869)
XLA Ops:
  11.1 44.1 %all-reduce.9 = bf16[2048]{0:T(1024)(128)(2,1)S(1)} all-reduce(bf16[2048]{0:T(1024)(128)(2,1)S(1)} %dynamic-update-slice), channel_id=1, replica_groups=mesh['dp'=16,'tensor'=2] {'dp','tensor'}, use_global_device_ids=true, to_apply=%add.9 | all-reduce | flops 2048 | bytes 8192
  57.6 73.3 %all_gather.27 = bf16[112,2048]{0,1:T(8,128)(2,1)S(1)} all-gather(bf16[112,64]{0,1:T(8,128)(2,1)} %param.31), channel_id=1, replica_groups=mesh['dp'=16,'tensor'=2] {'dp','tensor'}, dimensions={1}, use_global_device_ids=true | all-gather | bytes 473088 | tf_op jit(solution)/shard_map/all_gather | solution.py:151
  131.5 78.5 %all_gather.30 = bf16[2,2,2048]{1,0,2:T(2,128)(2,1)S(1)} all-gather(bf16[2,2,64]{1,0,2:T(2,128)(2,1)S(1)} %copy.173), channel_id=1, replica_groups=mesh['dp'=16,'tensor'=2] {'dp','tensor'}, dimensions={2}, use_global_device_ids=true | all-gather | bytes 16896 | tf_op jit(solution)/shard_map/all_gather | solution.py:154
  221.1 101.7 %while.32 = (s32[]{:T(128)}, f32[4,64,2048]{2,1,0:T(8,128)}, s32[4,64,50]{1,2,0:T(8,128)S(1)}, bf16[262,16]{0,1:T(8,128)(2,1)S(1)}, bf16[112,2048]{1,0:T(8,128)(...) while((s32[]{:T(128)}, f32[4,64,2048]{2,1,0:T(8,128)}, ...), condition=%wide.region_4.5_spmd.clone.clone, body=%wide.region_1.4_spmd.clone.sunk.clone | while | flops 1541675776 | bytes 60008220 | solution.py:167
  284.9 11.8 exponential_reduce_fusion.3
  335.8 23.5 %fusion.129 = (bf16[1,2048,2,2048]{1,3,2,0:T(8,128)(2,1)}, bf16[1,2048,2,2048]{1,3,2,0:T(8,128)(2,1)}) fusion(bf16[2,2048,2,2048]{1,3,2,0:T(8,128)(2,1)} %all-gather.3.cloned.1.call-done), kind=kLoop, calls=%fused_computation.285 | loop fusion | bytes 67108864 | tf_op jit(solution)/shard_map/slice | solution.py:74
  378.8 13.0 convolution_add_fusion
  423.6 17.8 reduce-scatter.14.cloned.1.call-done
  490.9 11.9 all_gather.34
  512.1 16.7 reduce-scatter.18.cloned.1.call-done
  561.6 17.3 reduce-scatter.20.cloned.1.call-done
  587.8 12.1 multiply_convert_fusion.4
  603.9 13.2 fusion.106
  626.2 33.7 %copy.190 = f32[1,2048,2,2048]{3,1,2,0:T(8,128)} copy(f32[1,2048,2,2048]{1,3,2,0:T(8,128)} %bitcast.286) | data formatting | bytes 67108864 | tf_op jit(solution)/shard_map/stack | solution.py:103
  660.0 13.2 convolution_bitcast_fusion.1
  673.1 44.0 %pad_maximum_fusion = f32[2,2048,2,2048]{3,1,2,0:T(8,128)} fusion(f32[1,2048,2,2048]{3,1,2,0:T(8,128)} %copy.190, f32[1,2048,2,2048]{3,1,2,0:T(8,128)} %convolution_bitcast_fusion.1), kind=kLoop, calls=%fused_computation.65 | loop fusion | flops 16777216 | bytes 134217728 | tf_op jit(solution)/shard_map/stack | solution.py:103
  717.1 97.5 %copy.191 = f32[2,2048,2,2048]{1,2,0,3:T(2,128)} copy(f32[2,2048,2,2048]{3,1,2,0:T(8,128)} %pad_maximum_fusion) | data formatting | bytes 134217728 | tf_op jit(solution)/shard_map/stack | solution.py:103
  817.7 14.5 fusion.49
  832.2 257.4 %while.33 = (s32[]{:T(128)}, f32[112,2048]{1,0:T(8,128)}, f32[2048]{0:T(1024)S(1)}, f32[262,16]{0,1:T(8,128)S(1)}, s32[4,64,50]{1,2,0:T(8,128)}, /*index=5*/bf16...) while((s32[]{:T(128)}, f32[112,2048]{1,0:T(8,128)}, ...), condition=%wide.region_25.26_spmd.clone.clone, body=%wide.region_21.25_spmd.clone.sunk.clone | while | flops 4558481408 | bytes 300154048 | solution.py:392
  847.5 12.2 fusion.224
  911.1 13.0 fusion.224
  975.3 12.3 fusion.224
  1039.4 13.2 fusion.224
  1113.5 65.4 %all-reduce.13 = (f32[2,384]{1,0:T(2,128)}, f32[1536]{0:T(1024)}) all-reduce(f32[2,384]{1,0:T(2,128)S(1)} %pad_maximum_fusion.7, f32[1536]{0:T(1024)S(1)} %copy-done.76), channel_id=1, replica_groups=mesh['dp'=16,'tensor'=2] {'dp'}, use_global_device_ids=true, to_apply=%region_38.39 | all-reduce | flops 2304 | bytes 18432 | tf_op jit(solution)/shard_map/psum | solution.py:340
  1179.0 41.8 %all-reduce.12 = (f32[262,16]{0,1:T(8,128)}, f32[2048]{0:T(1024)S(1)}, f32[768]{0:T(1024)}, f32[768]{0:T(1024)}, f32[768]{0:T(1024)}, /*index=5*/f32[768]{0:T(1024)}, f32[768]{0:T(1024)}, f32[768]{0:T(1024)}, f32[768]{0:T(1024)}) all-reduce(f32[262,16]{0,1:T(8,128)S(1)} %copy-done.52, ...), channel_id=1, replica_groups=mesh['dp'=16,'tensor'=2] {'dp','tensor'}, use_global_device_ids=true, to_apply=%region_26.27 | all-reduce | flops 11616 | bytes 92928 | tf_op jit(solution)/shard_map/psum | solution.py:414
  1222.9 565.4 %all-reduce.16.cloned.1.call-done = f32[2,2048,2,2048]{1,2,0,3:T(2,128)} async-done(((f32[2,2048,2,2048]{1,2,0,3:T(2,128)}), f32[2,2048,2,2048]{1,2,0,3:T(2,128)}) %all-reduce.16.cloned.1.call-update) | async-done | bytes 67108880
  1792.8 58.1 %reduce-scatter.28.cloned.1.call-done = f32[384,48]{0,1:T(8,128)} async-done(((f32[384,768]{0,1:T(8,128)}), f32[384,48]{0,1:T(8,128)}) %reduce-scatter.28.cloned.1.call-update) | async-done | bytes 73744 | tf_op jit(solution)/shard_map/reduce_scatter | solution.py:336
  1850.9 136.8 %reduce-scatter.22.cloned.1.call-done = f32[112,64]{0,1:T(8,128)} async-done(((f32[112,2048]{0,1:T(8,128)}), f32[112,64]{0,1:T(8,128)}) %reduce-scatter.22.cloned.1.call-update) | async-done | bytes 28688 | tf_op jit(solution)/shard_map/reduce_scatter | solution.py:399
  1987.8 68.5 %reduce-scatter.26.cloned.1.call-done = f32[48,3,384]{2,0,1:T(8,128)} async-done(((f32[768,3,384]{2,0,1:T(8,128)}), f32[48,3,384]{2,0,1:T(8,128)}) %reduce-scatter.26.cloned.1.call-update) | async-done | bytes 221200 | tf_op jit(solution)/shard_map/reduce_scatter | solution.py:335
  2056.3 78.8 %reduce-scatter.30.cloned.1.call-done = f32[48,1536]{1,0:T(8,128)} async-done(((f32[768,1536]{1,0:T(8,128)}), f32[48,1536]{1,0:T(8,128)}) %reduce-scatter.30.cloned.1.call-update) | async-done | bytes 294928 | tf_op jit(solution)/shard_map/reduce_scatter | solution.py:337
  2135.0 79.5 %reduce-scatter.32.cloned.1.call-done = f32[1536,48]{0,1:T(8,128)} async-done(((f32[1536,768]{0,1:T(8,128)}), f32[1536,48]{0,1:T(8,128)}) %reduce-scatter.32.cloned.1.call-update) | async-done | bytes 294928 | tf_op jit(solution)/shard_map/reduce_scatter | solution.py:338
  2214.6 119.4 %reduce-scatter.24.cloned.1.call-done = f32[64,768]{1,0:T(8,128)} async-done(((f32[2048,768]{1,0:T(8,128)}), f32[64,768]{1,0:T(8,128)}) %reduce-scatter.24.cloned.1.call-update) | async-done | bytes 196624 | tf_op jit(solution)/shard_map/reduce_scatter | solution.py:403
  (468 shorter events, 523.8 us)
Async XLA Ops:
  7.2 448.1 %copy-start = (bf16[768,1536]{1,0:T(8,128)(2,1)S(1)}, bf16[768,1536]{1,0:T(8,128)(2,1)}, u32[]{:S(2)}) copy-start(bf16[768,1536]{1,0:T(8,128)(2,1)} %param.43) | copy-start | bytes 7077892
  7.2 328.6 %all-gather.3.cloned.1.call-start = ((), (), s32[]{:S(2)}) async-start(), calls=%async_computation.11 | async-start | bytes 34603008 | tf_op jit(solution)/shard_map/all_gather | solution.py:153
  7.9 391.5 %all-gather.5.cloned.1.call-start = ((), (), s32[]{:S(2)}) async-start(), calls=%async_computation.12 | async-start | bytes 3244032 | tf_op jit(solution)/shard_map/all_gather | solution.py:155
  8.7 432.8 %reduce-scatter.14.cloned.1.call-start = ((), (), s32[]{:S(2)}) async-start(), calls=%async_computation.13 | async-start | bytes 1179648 | tf_op jit(solution)/shard_map/reduce_scatter | solution.py:215
  8.8 122.2 %copy-start.78 = (s32[112]{0:T(128)}, s32[112]{0:T(128)S(1)}, u32[]{:S(2)}) copy-start(s32[112]{0:T(128)S(1)} %and_select_fusion.1) | copy-start | bytes 1348
  335.8 23.5 %copy-start.10 = (bf16[4,64,2048]{2,1,0:T(8,128)(2,1)S(1)}, bf16[4,64,2048]{2,1,0:T(8,128)(2,1)}, u32[]{:S(2)}) copy-start(bf16[4,64,2048]{2,1,0:T(8,128)(2,1)} %get-tuple-element.614) | copy-start | bytes 3145732
  421.2 65.0 %reduce-scatter.16.cloned.1.call-start = ((), (), s32[]{:S(2)}) async-start(), calls=%async_computation.14 | async-start | bytes 1179648 | tf_op jit(solution)/shard_map/reduce_scatter | solution.py:231
  468.6 60.2 %reduce-scatter.18.cloned.1.call-start = ((), (), s32[]{:S(2)}) async-start(), calls=%async_computation.15 | async-start | bytes 1179648 | tf_op jit(solution)/shard_map/reduce_scatter | solution.py:265
  511.2 20.1 copy-start.61
  511.2 20.1 copy-start.65
  511.2 67.7 %reduce-scatter.20.cloned.1.call-start = ((), (), s32[]{:S(2)}) async-start(), calls=%async_computation.16 | async-start | bytes 1179648 | tf_op jit(solution)/shard_map/reduce_scatter | solution.py:326
  528.8 20.8 slice-start
  557.6 21.3 copy-start.29
  561.4 660.1 %reduce-scatter.34.cloned.1.call-start = ((), (), s32[]{:S(2)}) async-start(), calls=%async_computation.23 | async-start | bytes 1081344
  626.2 1162.2 %all-reduce.16.cloned.1.call-start = ((), (), s32[]{:S(2)}) async-start(), calls=%async_computation.24 | async-start | bytes 134217728
  626.2 33.7 %copy-start.11 = (bf16[4,64,2048]{2,1,0:T(8,128)(2,1)S(1)}, bf16[4,64,2048]{2,1,0:T(8,128)(2,1)}, u32[]{:S(2)}) copy-start(bf16[4,64,2048]{2,1,0:T(8,128)(2,1)} %get-tuple-element.614) | copy-start | bytes 3145732
  814.7 1036.2 %reduce-scatter.28.cloned.1.call-start = ((), (), s32[]{:S(2)}) async-start(), calls=%async_computation.20 | async-start | bytes 1253376 | tf_op jit(solution)/shard_map/reduce_scatter | solution.py:336
  817.5 1170.2 %reduce-scatter.22.cloned.1.call-start = ((), (), s32[]{:S(2)}) async-start(), calls=%async_computation.17 | async-start | bytes 1081344 | tf_op jit(solution)/shard_map/reduce_scatter | solution.py:399
  832.2 259.1 %copy-start.79 = (s32[112]{0:T(128)S(1)}, s32[112]{0:T(128)}, u32[]{:S(2)}) copy-start(s32[112]{0:T(128)} %copy-done.78) | copy-start | bytes 1348
  1092.7 963.6 %reduce-scatter.26.cloned.1.call-start = ((), (), s32[]{:S(2)}) async-start(), calls=%async_computation.19 | async-start | bytes 3760128 | tf_op jit(solution)/shard_map/reduce_scatter | solution.py:335
  1096.9 1038.2 %reduce-scatter.30.cloned.1.call-start = ((), (), s32[]{:S(2)}) async-start(), calls=%async_computation.21 | async-start | bytes 5013504 | tf_op jit(solution)/shard_map/reduce_scatter | solution.py:337
  1102.5 1112.0 %reduce-scatter.32.cloned.1.call-start = ((), (), s32[]{:S(2)}) async-start(), calls=%async_computation.22 | async-start | bytes 5013504 | tf_op jit(solution)/shard_map/reduce_scatter | solution.py:338
  1107.8 1226.2 %reduce-scatter.24.cloned.1.call-start = ((), (), s32[]{:S(2)}) async-start(), calls=%async_computation.18 | async-start | bytes 6488064 | tf_op jit(solution)/shard_map/reduce_scatter | solution.py:403
  1112.8 66.1 %copy-start.52 = (f32[262,16]{0,1:T(8,128)S(1)}, f32[262,16]{0,1:T(8,128)}, u32[]{:S(2)}) copy-start(f32[262,16]{0,1:T(8,128)} %copy-done.51) | copy-start | bytes 50308
  1112.8 66.1 %copy-start.67 = (f32[768]{0:T(1024)S(1)}, f32[768]{0:T(1024)}, u32[]{:S(2)}) copy-start(f32[768]{0:T(1024)} %get-tuple-element.518) | copy-start | bytes 9220
  1112.8 66.1 %copy-start.68 = (f32[768]{0:T(1024)S(1)}, f32[768]{0:T(1024)}, u32[]{:S(2)}) copy-start(f32[768]{0:T(1024)} %get-tuple-element.523) | copy-start | bytes 9220
  1112.8 66.1 %copy-start.69 = (f32[768]{0:T(1024)S(1)}, f32[768]{0:T(1024)}, u32[]{:S(2)}) copy-start(f32[768]{0:T(1024)} %get-tuple-element.573) | copy-start | bytes 9220
  1112.8 66.1 %copy-start.70 = (f32[768]{0:T(1024)S(1)}, f32[768]{0:T(1024)}, u32[]{:S(2)}) copy-start(f32[768]{0:T(1024)} %get-tuple-element.516) | copy-start | bytes 9220
  1112.9 66.1 %copy-start.71 = (f32[768]{0:T(1024)S(1)}, f32[768]{0:T(1024)}, u32[]{:S(2)}) copy-start(f32[768]{0:T(1024)} %get-tuple-element.521) | copy-start | bytes 9220
  1112.9 66.1 %copy-start.72 = (f32[768]{0:T(1024)S(1)}, f32[768]{0:T(1024)}, u32[]{:S(2)}) copy-start(f32[768]{0:T(1024)} %get-tuple-element.576) | copy-start | bytes 9220
  1112.9 66.1 %copy-start.73 = (f32[768]{0:T(1024)S(1)}, f32[768]{0:T(1024)}, u32[]{:S(2)}) copy-start(f32[768]{0:T(1024)} %get-tuple-element.579) | copy-start | bytes 9220
  1788.4 545.7 %copy-start.1 = (bf16[768,1536]{1,0:T(8,128)(2,1)S(1)}, bf16[768,1536]{1,0:T(8,128)(2,1)}, u32[]{:S(2)}) copy-start(bf16[768,1536]{1,0:T(8,128)(2,1)} %param.43) | copy-start | bytes 7077892
  (84 other events, 537.7 us)
Sparse Core Ops, SparseCore 0:
  11.1 222.6 all-gather.2
  236.7 59.7 all-gather.4
  421.3 20.1 reduce-scatter.13
  468.7 17.4 reduce-scatter.15
  511.3 17.4 reduce-scatter.17
  561.5 17.4 reduce-scatter.19
  626.3 134.8 reduce-scatter.33
  814.8 973.5 all-reduce.15
  1793.0 57.9 reduce-scatter.27
  1853.7 134.0 reduce-scatter.21
  1992.2 63.9 reduce-scatter.25
  2060.6 74.4 reduce-scatter.29
  2140.0 74.5 reduce-scatter.31
  2220.6 113.3 reduce-scatter.23
where the time goes:
time: 2350 us; the launch traced here: 2340 us
  waiting for transfers between devices  1170 us (50%)
  blocking collectives  347 us (15%)
  matrix products  302 us (13%)
  local copies, waits for them, and re-layouts  256 us (11%)
  other arithmetic  248 us (11%)
    unnamed x16, waiting for transfers between devices  567 us
    reduce_scatter x1, waiting for transfers between devices, per_device(): lax.psum_scatter(conv_weight_total, ('dp', 'tensor'), scatter_dimension=1...  137 us
    another operation x4, local copies, waits for them, and re-layouts, highway_backward(): return (grad_state, jnp.stack(weight_grads), jnp.stack(bias_grads))  131 us
    reduce_scatter x1, waiting for transfers between devices, per_device(): lax.psum_scatter(proj_grad, ('dp', 'tensor'), scatter_dimension=0, tiled=...  119 us
    reduce_sum x8, other arithmetic, conv_pool(): exp_total = jnp.sum(exp_terms, axis=1, keepdims=True)  97.4 us
    dot_general x8, matrix products, conv_pool(): jnp.einsum('wcr,rf->wcf', windows, conv_masked, preferred_element_type=jn...  86.5 us
    reduce_scatter x1, waiting for transfers between devices, per_device(): lax.psum_scatter(down_weight_grad, 'dp', scatter_dimension=1, tiled=True)  79.5 us
    reduce_scatter x1, waiting for transfers between devices, per_device(): lax.psum_scatter(up_weight_grad, 'dp', scatter_dimension=0, tiled=True)  78.8 us
  transfers between devices with their start and end apart: 14, of which 11 were waited for; matrix products, arithmetic and copies ran while one was open for 28% of the time, Pallas kernels for 0%

commit v1 on v0

v1 whole, which is shorter than its diff:
```python
import functools
import math

import jax
import jax.numpy as jnp
from jax import lax
from jax.experimental import pallas as pl
from jax.experimental.pallas import tpu as pltpu
from jax.sharding import PartitionSpec as P

HEAD_DIM = 64
FILTERS = 2048
CHAR_DIM = 16
CHARS = 50
MAX_WIDTH = 7
LEN = 512
D = 768

channel_shares = (1, 2, 4, 8, 16, 32)
norm_eps = 1e-05
big_negative = -1e30
f32 = jnp.float32
bf16 = jnp.bfloat16
PAIR = "tensor"
GROUP = "dp"
TAPS = 128
VROWS = (CHARS + 7) * CHAR_DIM
FBLOCK = 256


def gelu(x):
    return jax.nn.gelu(x, approximate=False)


def gelu_slope(x):
    return 0.5 * (1.0 + lax.erf(x * (1.0 / math.sqrt(2.0)))) + x * jnp.exp(-0.5 * x * x) * (
        1.0 / math.sqrt(2.0 * math.pi)
    )


def width_of(channel):
    return 1 + sum(channel >= part * (FILTERS // 64) for part in channel_shares)


def dot(a, b, ca, cb):
    return lax.dot_general(a, b, (((ca,), (cb,)), ((), ())), preferred_element_type=f32)


def block_limits(per, start, stop):
    widths = [
        width_of((row // per) * 2 * per + side * per + row % per)
        for row in range(start, stop)
        for side in range(2)
    ]
    return CHARS + 1 - max(widths), CHARS + 1 - min(widths)


MESH = pl.DeviceIdType.MESH
ANYWHERE = pl.BlockSpec(memory_space=pl.ANY)


def pair_swap(x):
    return lax.ppermute(x, PAIR, [(0, 1), (1, 0)])


class Place:
    def __init__(self, lines):
        self.lines = lines
        index = lax.axis_index(GROUP)
        self.side = lax.axis_index(PAIR)
        self.line, self.row, self.core = index // 4, (index // 2) % 2, index % 2
        self.sibling = self.at(self.line, self.row, 1 - self.core)
        self.across = self.at(self.line, 1 - self.row, self.core)
        self.partner = (index, 1 - self.side)

    def at(self, line, row, core):
        return ((line * 2 + row) * 2 + core, self.side)

    def on_line(self, line):
        return self.at(line, self.row, self.core)


def send(source, target, sems, device):
    copy = pltpu.make_async_remote_copy(
        src_ref=source, dst_ref=target, send_sem=sems[0], recv_sem=sems[1],
        device_id=device, device_id_type=MESH,
    )
    copy.start()
    return copy


def meet(devices):
    barrier = pltpu.get_barrier_semaphore()
    for device in devices:
        pl.semaphore_signal(barrier, inc=1, device_id=device, device_id_type=MESH)
    pl.semaphore_wait(barrier, len(devices))


class Gather:
    def __init__(self, place, blocks, wholes, sems):
        self.place, self.blocks, self.wholes = place, blocks, wholes
        self.line_s, self.line_r, self.row_s, self.row_r, self.core_s, self.core_r, self.own = sems

    def piece(self, k, line, row, core):
        return self.wholes[k].at[line, row, core]

    def to_line(self, k, source, line, step):
        p = self.place
        return pltpu.make_async_remote_copy(
            src_ref=source, dst_ref=self.piece(k, line, p.row, p.core),
            send_sem=self.line_s.at[k, line, 0 if step > 0 else 1], recv_sem=self.line_r.at[k, line],
            device_id=p.on_line(lax.rem(p.line + step + p.lines, p.lines)), device_id_type=MESH,
        )

    def to_row(self, k, source, line):
        p = self.place
        return pltpu.make_async_remote_copy(
            src_ref=source, dst_ref=self.piece(k, line, p.row, p.core),
            send_sem=self.row_s.at[k, line], recv_sem=self.row_r.at[k, line],
            device_id=p.across, device_id_type=MESH,
        )

    def to_core(self, k, source, line, row):
        p = self.place
        return pltpu.make_async_remote_copy(
            src_ref=source, dst_ref=self.piece(k, line, row, p.core),
            send_sem=self.core_s.at[k, line, row], recv_sem=self.core_r.at[k, line, row],
            device_id=p.sibling, device_id_type=MESH,
        )

    def pass_on(self, k, line, source, left, right):
        p = self.place
        if right:
            @pl.when(p.line < p.lines - 1)
            def _():
                self.to_line(k, source, line, 1).start()
        if left:
            @pl.when(p.line > 0)
            def _():
                self.to_line(k, source, line, -1).start()
        self.to_row(k, source, line).start()
        self.to_core(k, source, line, p.row).start()

    def begin(self, k):
        p = self.place
        pltpu.make_async_copy(self.blocks[k], self.piece(k, p.line, p.row, p.core), self.own.at[k]).start()
        self.pass_on(k, p.line, self.blocks[k], True, True)

    def from_row(self, k, line):
        p = self.place
        got = self.piece(k, line, 1 - p.row, p.core)
        pltpu.make_async_remote_copy(
            src_ref=got, dst_ref=got, send_sem=self.row_s.at[k, line], recv_sem=self.row_r.at[k, line],
            device_id=p.across, device_id_type=MESH,
        ).wait_recv()
        self.to_core(k, got, line, 1 - p.row).start()

    def turn(self, k, r):
        p = self.place
        for step in (1, -1):
            line = p.line - step * r
            inside = (line >= 0) & (line < p.lines)

            @pl.when(inside)
            def _(line=line, step=step):
                got = self.piece(k, line, p.row, p.core)
                self.to_line(k, got, line, step).wait_recv()
                self.pass_on(k, line, got, step < 0, step > 0)
        self.crossed(k, r - 1)

    def crossed(self, k, r):
        p = self.place
        for step in (1, -1) if r else (1,):
            line = p.line - step * r
            inside = (line >= 0) & (line < p.lines)

            @pl.when(inside)
            def _(line=line):
                self.from_row(k, line)

    def finish(self, k):
        p = self.place
        self.crossed(k, p.lines - 1)
        own = self.piece(k, p.line, p.row, p.core)
        pltpu.make_async_copy(self.blocks[k], own, self.own.at[k]).wait()

        def each(line, carry):
            for row in range(2):
                self.to_core(k, self.piece(k, line, row, p.core), line, row).wait_send()
                self.to_core(k, self.piece(k, line, row, 1 - p.core), line, row).wait_recv()
            self.to_row(k, self.piece(k, line, p.row, p.core), line).wait_send()

            @pl.when((p.line < p.lines - 1) & (line <= p.line))
            def _():
                self.to_line(k, self.piece(k, line, p.row, p.core), line, 1).wait_send()

            @pl.when((p.line > 0) & (line >= p.line))
            def _():
                self.to_line(k, self.piece(k, line, p.row, p.core), line, -1).wait_send()
            return carry

        lax.fori_loop(0, p.lines, each, 0)

    @staticmethod
    def sems(count, lines):
        dma = pltpu.SemaphoreType.DMA
        return [
            dma((count, lines, 2)), dma((count, lines)), dma((count, lines)), dma((count, lines)),
            dma((count, lines, 2)), dma((count, lines, 2)), dma((count,)),
        ]


def neighbours(place, partner):
    others = [
        place.on_line(lax.rem(place.line + step, place.lines)) for step in range(1, place.lines)
    ]
    return [place.sibling, place.across, *others] + ([place.partner] if partner else [])


def gather_kernel(lines, count, swap, *refs):
    blocks, refs = refs[:count], refs[count:]
    swap_in, refs = refs[:swap], refs[swap:]
    wholes, refs = refs[:count], refs[count:]
    swap_out, refs = refs[:swap], refs[swap:]
    place = Place(lines)
    gather = Gather(place, blocks, wholes, refs[:7])
    meet(neighbours(place, bool(swap)))
    for k in range(count):
        gather.begin(k)
    if swap:
        copy = send(swap_in[0], swap_out[0], refs[7:9], place.partner)
    for r in range(1, lines):
        for k in range(count):
            gather.turn(k, r)
    for k in range(count):
        gather.finish(k)
    if swap:
        copy.wait()


def gather_blocks(blocks, lines, ident, swap=None):
    count = len(blocks)
    swaps = [] if swap is None else [swap]
    dma = pltpu.SemaphoreType.DMA
    outs = pl.pallas_call(
        functools.partial(gather_kernel, lines, count, len(swaps)),
        out_shape=tuple(
            [jax.ShapeDtypeStruct((lines, 2, 2) + b.shape, b.dtype) for b in blocks]
            + [jax.ShapeDtypeStruct(s.shape, s.dtype) for s in swaps]
        ),
        in_specs=[ANYWHERE] * (count + len(swaps)),
        out_specs=tuple([ANYWHERE] * (count + len(swaps))),
        scratch_shapes=Gather.sems(count, lines) + [dma, dma] * len(swaps),
        compiler_params=pltpu.CompilerParams(collective_id=ident, has_side_effects=True),
    )(*blocks, *swaps)
    return [o.reshape((4 * lines,) + b.shape) for o, b in zip(outs, blocks)] + list(outs[count:])


class Scatter:
    def __init__(self, place, arrays, from_core, from_row, from_line, outs, pieces, bufs, sems):
        self.place, self.arrays, self.outs, self.pieces = place, arrays, outs, pieces
        self.from_core, self.from_row, self.from_line = from_core, from_row, from_line
        self.mine, self.theirs, self.sums, self.crossed, self.leaving, self.arrived = bufs
        self.core_s, self.core_r, self.row_s, self.row_r, self.line_s, self.line_r, self.load = sems

    def span(self, k):
        array, start, size = self.pieces[k]
        return array, pl.ds(start, size), size, self.arrays[array].shape[-1]

    def core_copy(self, k):
        array, rows, size, width = self.span(k)
        p = self.place
        return pltpu.make_async_remote_copy(
            src_ref=self.arrays[array].at[:, :, 1 - p.core, rows],
            dst_ref=self.from_core[array].at[:, :, rows],
            send_sem=self.core_s.at[k], recv_sem=self.core_r.at[k],
            device_id=p.sibling, device_id_type=MESH,
        )

    def row_copy(self, k):
        array, rows, size, width = self.span(k)
        p = self.place
        return pltpu.make_async_remote_copy(
            src_ref=self.sums.at[k % self.sums.shape[0], 1 - p.row, :, pl.ds(0, size), pl.ds(0, width)],
            dst_ref=self.from_row[array].at[:, rows],
            send_sem=self.row_s.at[k], recv_sem=self.row_r.at[k],
            device_id=p.across, device_id_type=MESH,
        )

    def line_copy(self, k, step):
        array, rows, size, width = self.span(k)
        p = self.place
        line = lax.rem(p.line + step, p.lines)
        return pltpu.make_async_remote_copy(
            src_ref=self.leaving.at[k % self.leaving.shape[0], line, pl.ds(0, size), pl.ds(0, width)],
            dst_ref=self.from_line[array].at[step, rows],
            send_sem=self.line_s.at[k, step], recv_sem=self.line_r.at[k, step],
            device_id=p.on_line(line), device_id_type=MESH,
        )

    def begin(self, k):
        self.core_copy(k).start()

    def add_core(self, k):
        array, rows, size, width = self.span(k)
        p = self.place
        slot = k % self.sums.shape[0]
        if k >= self.sums.shape[0]:
            self.row_copy(k - self.sums.shape[0]).wait_send()
        here = (slice(None), slice(None), pl.ds(0, size), pl.ds(0, width))
        mine = pltpu.make_async_copy(
            self.arrays[array].at[:, :, p.core, rows], self.mine.at[here], self.load.at[0]
        )
        mine.start()
        self.core_copy(k).wait_recv()
        theirs = pltpu.make_async_copy(
            self.from_core[array].at[:, :, rows], self.theirs.at[here], self.load.at[1]
        )
        theirs.start()
        mine.wait()
        theirs.wait()

        def each(i, carry):
            line = i // (size // 16)
            part = pl.ds(pl.multiple_of((i % (size // 16)) * 16, 16), 16)
            for row in range(2):
                total = self.mine[line, row, part, :width].astype(f32) + self.theirs[
                    line, row, part, :width
                ].astype(f32)
                self.sums[slot, row, line, part, :width] = total.astype(bf16)
            return carry

        lax.fori_loop(0, p.lines * (size // 16), each, 0)
        self.row_copy(k).start()

    def add_row(self, k):
        array, rows, size, width = self.span(k)
        p = self.place
        slot = k % self.sums.shape[0]
        away = k % self.leaving.shape[0]
        if k >= self.leaving.shape[0]:
            for step in range(1, p.lines):
                self.line_copy(k - self.leaving.shape[0], step).wait_send()
        here = (slice(None), pl.ds(0, size), pl.ds(0, width))
        self.row_copy(k).wait_recv()
        copy = pltpu.make_async_copy(
            self.from_row[array].at[:, rows], self.crossed.at[here], self.load.at[2]
        )
        copy.start()
        copy.wait()

        def each(i, carry):
            line = i // (size // 16)
            part = pl.ds(pl.multiple_of((i % (size // 16)) * 16, 16), 16)
            total = self.sums[slot, p.row, line, part, :width].astype(f32) + self.crossed[
                line, part, :width
            ].astype(f32)
            self.leaving[away, line, part, :width] = total.astype(bf16)
            return carry

        lax.fori_loop(0, p.lines * (size // 16), each, 0)
        for step in range(1, p.lines):
            self.line_copy(k, step).start()
        own = self.leaving.at[away, p.line, pl.ds(0, size), pl.ds(0, width)]
        copy = pltpu.make_async_copy(own, self.from_line[array].at[0, rows], self.load.at[3])
        copy.start()
        copy.wait()

    def add_line(self, k):
        array, rows, size, width = self.span(k)
        start = self.pieces[k][1]
        p = self.place
        for step in range(1, p.lines):
            self.line_copy(k, step).wait_recv()
        here = (slice(None), pl.ds(0, size), pl.ds(0, width))
        copy = pltpu.make_async_copy(
            self.from_line[array].at[:, rows], self.arrived.at[here], self.load.at[4]
        )
        copy.start()
        copy.wait()

        def each(i, carry):
            part = pl.ds(pl.multiple_of(i * 16, 16), 16)
            total = self.arrived[0, part, :width].astype(f32)
            for step in range(1, p.lines):
                total = total + self.arrived[step, part, :width].astype(f32)
            self.outs[array][pl.ds(pl.multiple_of(start + i * 16, 16), 16), :] = total
            return carry

        lax.fori_loop(0, size // 16, each, 0)

    def steps(self):
        count = len(self.pieces)
        work = []
        for k in range(count + 4):
            if k < count:
                work.append(functools.partial(self.add_core, k))
            if 0 <= k - 2 < count:
                work.append(functools.partial(self.add_row, k - 2))
            if 0 <= k - 4 < count:
                work.append(functools.partial(self.add_line, k - 4))
        return work

    def finish(self):
        count = len(self.pieces)
        for k in range(count):
            self.core_copy(k).wait_send()
            if k >= count - self.sums.shape[0]:
                self.row_copy(k).wait_send()
            if k >= count - self.leaving.shape[0]:
                for step in range(1, self.place.lines):
                    self.line_copy(k, step).wait_send()

    @staticmethod
    def shapes(arrays, pieces, lines):
        land = []
        for lead in ((lines, 2), (lines,), (lines,)):
            land += [jax.ShapeDtypeStruct(lead + a.shape[3:], bf16) for a in arrays]
        outs = [jax.ShapeDtypeStruct(a.shape[3:], f32) for a in arrays]
        rows = max(size for _, _, size in pieces)
        width = max(a.shape[-1] for a in arrays)
        dma = pltpu.SemaphoreType.DMA
        count = len(pieces)
        bufs = [
            pltpu.VMEM((lines, 2, rows, width), bf16), pltpu.VMEM((lines, 2, rows, width), bf16),
            pltpu.VMEM((3, 2, lines, rows, width), bf16), pltpu.VMEM((lines, rows, width), bf16),
            pltpu.VMEM((2, lines, rows, width), bf16), pltpu.VMEM((lines, rows, width), bf16),
        ]
        sems = [dma((count,))] * 4 + [dma((count, lines))] * 2 + [dma((5,))]
        return land, outs, bufs, sems


def scatter_kernel(lines, count, pieces, swap, *refs):
    arrays, refs = refs[:count], refs[count:]
    swap_in, refs = refs[:swap], refs[swap:]
    land, refs = refs[: 3 * count], refs[3 * count :]
    outs, refs = refs[:count], refs[count:]
    swap_out, refs = refs[:swap], refs[swap:]
    place = Place(lines)
    scatter = Scatter(
        place, arrays, land[:count], land[count : 2 * count], land[2 * count :], outs, pieces,
        refs[:6], refs[6:13],
    )
    meet(neighbours(place, bool(swap)))
    if swap:
        copy = send(swap_in[0], swap_out[0], refs[13:15], place.partner)
    for k in range(len(pieces)):
        scatter.begin(k)
    for step in scatter.steps():
        step()
    scatter.finish()
    if swap:
        copy.wait()


def cut(arrays, most):
    pieces = []
    for i, a in enumerate(arrays):
        rows = a.shape[3]
        size = max(s for s in range(16, most + 1, 16) if rows % s == 0)
        pieces += [(i, start, size) for start in range(0, rows, size)]
    return pieces


def scatter_blocks(arrays, lines, ident, most=48, swap=None):
    whole = []
    for a in arrays:
        rows = -(-a.shape[1] // 16) * 16
        a = jnp.pad(a.astype(bf16), ((0, 0), (0, rows - a.shape[1]), (0, 0)))
        whole.append(a.reshape((lines, 2, 2) + a.shape[1:]))
    pieces = cut(whole, most)
    land, outs, bufs, sems = Scatter.shapes(whole, pieces, lines)
    swaps = [] if swap is None else [swap]
    dma = pltpu.SemaphoreType.DMA
    count = len(arrays)
    result = pl.pallas_call(
        functools.partial(scatter_kernel, lines, count, pieces, len(swaps)),
        out_shape=tuple(land + outs + [jax.ShapeDtypeStruct(s.shape, s.dtype) for s in swaps]),
        in_specs=[ANYWHERE] * (count + len(swaps)),
        out_specs=tuple(
            [ANYWHERE] * len(land)
            + [pl.BlockSpec(memory_space=pltpu.VMEM)] * count
            + [ANYWHERE] * len(swaps)
        ),
        scratch_shapes=bufs + sems + [dma, dma] * len(swaps),
        compiler_params=pltpu.CompilerParams(
            collective_id=ident, has_side_effects=True, vmem_limit_bytes=48 << 20
        ),
    )(*whole, *swaps)
    own = [r[: a.shape[1]] for r, a in zip(result[3 * count : 4 * count], arrays)]
    return own + list(result[4 * count :])


def total_kernel(lines, x_ref, o_ref, inbox, send_sems, recv_sems):
    place = Place(lines)
    partners = [place.sibling, place.across]
    span = 1
    while span < lines:
        low = lax.rem(place.line // span, 2)
        partners.append(place.on_line(place.line + span - 2 * span * low))
        span *= 2
    partners.append(place.partner)
    meet(partners)
    o_ref[...] = x_ref[...]
    for i, device in enumerate(partners):
        copy = send(o_ref, inbox.at[i], (send_sems.at[i], recv_sems.at[i]), device)
        copy.wait()
        o_ref[...] = o_ref[...] + inbox[i]


def total_all(x, lines, ident):
    count = 3 + (lines - 1).bit_length()
    dma = pltpu.SemaphoreType.DMA
    vmem = pl.BlockSpec(memory_space=pltpu.VMEM)
    return pl.pallas_call(
        functools.partial(total_kernel, lines),
        out_shape=jax.ShapeDtypeStruct(x.shape, x.dtype),
        in_specs=[vmem],
        out_specs=vmem,
        scratch_shapes=[pltpu.VMEM((count,) + x.shape, x.dtype), dma((count,)), dma((count,))],
        compiler_params=pltpu.CompilerParams(collective_id=ident, has_side_effects=True),
    )(x)


def onehot_chars(ids_row, count):
    return jnp.where(
        lax.broadcasted_iota(jnp.int32, (count, ids_row.shape[1]), 0) == ids_row, 1.0, 0.0
    ).astype(bf16)


def conv_forward_kernel(limits, ids_ref, table_ref, weight_ref, lim_ref, pooled_ref, chars_ref, conv_ref):
    words = ids_ref.shape[1]
    count = table_ref.shape[1]

    def embed(c, carry):
        hot = onehot_chars(ids_ref[pl.ds(c, 1), :], count)
        vec = dot(table_ref[...], hot, 1, 0)
        chars_ref[pl.ds(pl.multiple_of(c * CHAR_DIM, CHAR_DIM), CHAR_DIM), :] = vec.astype(bf16)
        return carry

    lax.fori_loop(0, CHARS, embed, 0)
    chars_ref[CHARS * CHAR_DIM :, :] = jnp.zeros((VROWS - CHARS * CHAR_DIM, words), bf16)

    for block, (full, some) in enumerate(limits):
        rows = pl.ds(block * FBLOCK, FBLOCK)
        for half in range(words // FBLOCK):
            lanes = pl.ds(half * FBLOCK, FBLOCK)

            def convolve(p, carry):
                taps = chars_ref[pl.ds(pl.multiple_of(p * CHAR_DIM, CHAR_DIM), TAPS), lanes]
                conv_ref[p] = dot(weight_ref[rows, :], taps, 1, 0)
                return carry

            lax.fori_loop(0, some, convolve, 0)

            def pool(g, carry):
                here = pl.ds(pl.multiple_of(g * 8, 8), 8)
                there = pl.ds(pl.multiple_of(block * FBLOCK + g * 8, 8), 8)
                lim = lim_ref[there, :] if some > full else None

                def entry(p):
                    value = conv_ref[p, here, :]
                    return value if p < full else jnp.where(lim[:, :1] >= p, value, big_negative)

                top = entry(0)
                for p in range(1, some):
                    top = jnp.maximum(top, entry(p))
                total = jnp.exp(entry(0) - top)
                for p in range(1, some):
                    total = total + jnp.exp(entry(p) - top)
                pooled_ref[there, lanes] = top + jnp.log(total)
                return carry

            lax.fori_loop(0, FBLOCK // 8, pool, 0)


def conv_forward(ids, table, weight, lim, per):
    rows = weight.shape[0]
    words = ids.shape[1]
    limits = tuple(block_limits(per, s, s + FBLOCK) for s in range(0, rows, FBLOCK))
    return pl.pallas_call(
        functools.partial(conv_forward_kernel, limits),
        out_shape=(
            jax.ShapeDtypeStruct((rows, words), f32),
            jax.ShapeDtypeStruct((VROWS, words), bf16),
        ),
        scratch_shapes=[pltpu.VMEM((CHARS, FBLOCK, FBLOCK), f32)],
        compiler_params=pltpu.CompilerParams(vmem_limit_bytes=48 << 20),
        cost_estimate=pl.CostEstimate(flops=14 * 10**9, bytes_accessed=8 << 20, transcendentals=24 * 10**6),
    )(ids, table, weight, lim)


def conv_backward_kernel(
    limits, ids_ref, chars_ref, weight_ref, weight_t_ref, lim_ref, pooled_ref, grad_ref,
    weight_grad_ref, table_grad_ref, dconv_ref, dchars_ref,
):
    words = ids_ref.shape[1]
    count = table_grad_ref.shape[1]
    dchars_ref[...] = jnp.zeros_like(dchars_ref)
    weight_grad_ref[...] = jnp.zeros_like(weight_grad_ref)
    table_grad_ref[...] = jnp.zeros_like(table_grad_ref)
    always = min(full for full, some in limits)
    ever = max(some for full, some in limits)

    def place(p, blocks):
        if isinstance(p, int):
            window = pl.ds(p * CHAR_DIM, TAPS)
        else:
            window = pl.ds(pl.multiple_of(p * CHAR_DIM, CHAR_DIM), TAPS)
        for block in blocks:
            full, some = limits[block]
            rows = pl.ds(block * FBLOCK, FBLOCK)
            taps = chars_ref[window, :]
            weights = jnp.exp(dot(weight_ref[rows, :], taps, 1, 0) - pooled_ref[rows, :])
            value = weights * grad_ref[rows, :]
            if isinstance(p, int) and p >= full:
                value = jnp.where(lim_ref[rows, :][:, :1] >= p, value, 0.0)
            value = value.astype(bf16)
            dconv_ref[rows, :] = value
            weight_grad_ref[rows, :] += dot(value, taps, 1, 1)
        count_rows = len(blocks) * FBLOCK
        dchars_ref[window, :] += dot(weight_t_ref[:, :count_rows], dconv_ref[:count_rows, :], 1, 0)

    everyone = range(len(limits))

    def step(p, carry):
        place(p, everyone)
        return carry

    lax.fori_loop(0, always, step, 0)
    for p in range(always, ever):
        blocks = [block for block, (full, some) in enumerate(limits) if p < some]
        place(p, range(max(blocks) + 1))

    def spread(c, carry):
        rows = pl.ds(pl.multiple_of(c * CHAR_DIM, CHAR_DIM), CHAR_DIM)
        hot = onehot_chars(ids_ref[pl.ds(c, 1), :], count)
        table_grad_ref[...] += dot(dchars_ref[rows, :].astype(bf16), hot, 1, 1)
        return carry

    lax.fori_loop(0, CHARS, spread, 0)


def conv_backward(ids, chars, weight, lim, pooled, grad, per, count):
    rows = weight.shape[0]
    words = ids.shape[1]
    limits = tuple(block_limits(per, s, s + FBLOCK) for s in range(0, rows, FBLOCK))
    return pl.pallas_call(
        functools.partial(conv_backward_kernel, limits),
        out_shape=(
            jax.ShapeDtypeStruct((rows, TAPS), f32),
            jax.ShapeDtypeStruct((CHAR_DIM, count), f32),
        ),
        scratch_shapes=[pltpu.VMEM((rows, words), bf16), pltpu.VMEM((VROWS, words), f32)],
        compiler_params=pltpu.CompilerParams(vmem_limit_bytes=48 << 20),
        cost_estimate=pl.CostEstimate(flops=42 * 10**9, bytes_accessed=8 << 20, transcendentals=24 * 10**6),
    )(ids, chars, weight, weight.T, lim, pooled, grad)


def norm_forward(summed):
    centred = summed - jnp.mean(summed, axis=-1, keepdims=True)
    inv_std = lax.rsqrt(jnp.mean(centred * centred, axis=-1, keepdims=True) + norm_eps)
    return centred * inv_std, inv_std


def norm_backward(grad_out, normalized, inv_std, gain):
    grad_norm = grad_out * gain
    return inv_std * (
        grad_norm
        - jnp.mean(grad_norm, axis=-1, keepdims=True)
        - normalized * jnp.mean(grad_norm * normalized, axis=-1, keepdims=True)
    )


def split_two(x):
    high = x.astype(bf16)
    return high, (x - high.astype(f32)).astype(bf16)


def per_device(
    char_ids, mask_pos, out_grad, char_table, conv_weight, conv_bias, highway_weight, highway_bias,
    proj_weight, proj_bias, qkv_weight, qv_bias, out_weight, out_bias, ln1_gain, ln1_bias, up_weight,
    up_bias, down_weight, down_bias, ln2_gain, ln2_bias,
):
    side = lax.axis_index(PAIR)
    per = conv_weight.shape[1]
    ndp = FILTERS // (2 * per)
    rows_here = char_ids.shape[0]
    words = 2 * rows_here
    own = ndp * per
    layers = highway_weight.shape[0]
    ids_count = char_table.shape[0]
    padded_ids = -(-ids_count // 128) * 128

    taps_used = conv_weight.shape[0]
    packed = jnp.concatenate(
        [
            conv_weight.T.astype(f32),
            conv_bias[:, None].astype(f32),
            highway_bias.reshape(2 * layers, per).T.astype(f32),
            jnp.zeros((per, TAPS - taps_used - 1 - 2 * layers), f32),
        ],
        axis=1,
    )
    highway_t = highway_weight.transpose(0, 2, 3, 1)
    lines = ndp // 4
    blocks = [highway_t[i].reshape(2 * per, FILTERS) for i in range(layers)]
    highway_all = [None] * layers
    packed_all, highway_all[0] = gather_blocks([packed, blocks[0]], lines, 1)
    packed_all = packed_all.reshape(own, TAPS)
    highway_all[0] = highway_all[0].reshape(2 * own, FILTERS)

    filter_index = jnp.arange(own, dtype=jnp.int32)
    filter_index = (filter_index // per) * (2 * per) + side * per + filter_index % per
    filter_width = width_of(filter_index).astype(jnp.int32)
    lim = jnp.broadcast_to((CHARS - filter_width)[:, None], (own, 128))
    tap_shift = jnp.arange(TAPS, dtype=jnp.int32) // CHAR_DIM
    conv_all = jnp.where(
        (tap_shift[None, :] < filter_width[:, None]) & (jnp.arange(TAPS) < taps_used)[None, :],
        packed_all,
        0.0,
    ).astype(bf16)
    conv_bias_all = packed_all[:, taps_used][:, None]

    def layer_bias(i):
        both = packed_all[:, taps_used + 1 + 2 * i : taps_used + 3 + 2 * i]
        return both.reshape(ndp, per, 2).transpose(0, 2, 1)[..., None]

    def both_sides(mine, theirs):
        mine = mine.reshape(ndp, 1, per, words)
        theirs = theirs.reshape(ndp, 1, per, words)
        first = jnp.where(side == 0, mine, theirs)
        second = jnp.where(side == 0, theirs, mine)
        return jnp.concatenate([first, second], axis=1).reshape(FILTERS, words)

    ids = lax.all_gather(char_ids.T, PAIR, axis=1, tiled=True)
    table_t = jnp.pad(char_table.T, ((0, 0), (0, padded_ids - ids_count)))
    pooled_raw, chars = conv_forward(ids, table_t, conv_all, lim, per)
    pooled = pooled_raw + conv_bias_all
    state = gelu(pooled)
    kept = []
    for i in range(layers):
        state_low = state.astype(bf16)
        if i == 0:
            *highways, proj_all, other_low = gather_blocks(
                blocks[1:] + [proj_weight], lines, 2, state_low
            )
            highway_all[1:] = [h.reshape(2 * own, FILTERS) for h in highways]
            proj_all = proj_all.reshape(own, D)
        else:
            other_low = pair_swap(state_low)
        state_full = both_sides(state_low, other_low)
        pre = dot(highway_all[i], state_full, 1, 0).reshape(ndp, 2, per, words) + layer_bias(i)
        nonlin = pre[:, 0].reshape(own, words)
        gate = jax.nn.sigmoid(pre[:, 1].reshape(own, words))
        kept.append((state, state_full, nonlin, gate))
        state = gate * state + (1.0 - gate) * gelu(nonlin)
    state_low = state.astype(bf16)
    emb_part = dot(state_low, proj_all, 0, 0)
    embedded = emb_part + pair_swap(emb_part.astype(bf16)).astype(f32) + proj_bias.astype(f32)

    emb_low = embedded.astype(bf16)
    seqs = words // LEN
    width = qkv_weight.shape[2]
    heads = width // HEAD_DIM
    qkv_t = qkv_weight.transpose(1, 0, 2)
    qkv_bias = jnp.stack([qv_bias[0], jnp.zeros_like(qv_bias[0]), qv_bias[1]]).astype(f32)
    projected = [
        (dot(emb_low, qkv_t[part], 1, 0) + qkv_bias[part][None]).astype(bf16) for part in range(3)
    ]

    def by_head(x):
        return x.reshape(-1, heads, HEAD_DIM).transpose(1, 0, 2)

    queries, keys, values = (by_head(part) for part in projected)
    scale = 1.0 / math.sqrt(HEAD_DIM)

    def probs_of(q):
        scores = jnp.einsum("hqd,hkd->hqk", q, keys, preferred_element_type=f32) * scale
        terms = jnp.exp(scores - jnp.max(scores, axis=-1, keepdims=True))
        return terms / jnp.sum(terms, axis=-1, keepdims=True)

    mixed = (
        jnp.einsum("hqk,hkd->qhd", probs_of(queries).astype(bf16), values, preferred_element_type=f32)
        .reshape(words, width)
        .astype(bf16)
    )
    att_part = dot(mixed, out_weight, 1, 0)
    gain_one, gain_two = ln1_gain.astype(f32), ln2_gain.astype(f32)
    summed = embedded + (
        att_part + pair_swap(att_part.astype(bf16)).astype(f32) + out_bias.astype(f32)
    )
    normalized_one, inv_std_one = norm_forward(summed)
    normed = normalized_one * gain_one + ln1_bias.astype(f32)
    normed_low = normed.astype(bf16)
    hidden = gelu(dot(normed_low, up_weight, 1, 0) + up_bias.astype(f32)).astype(bf16)
    ffn_part = dot(hidden, down_weight, 1, 0)

    slots = mask_pos.shape[1]
    padded_slots = -(-slots // 16) * 16
    positions = jnp.pad(mask_pos[0], (0, padded_slots - slots), constant_values=-1)
    pick = (positions[:, None] == jnp.arange(words, dtype=jnp.int32)[None, :]).astype(bf16)
    slot_grad = jnp.pad(out_grad[0], ((0, padded_slots - slots), (0, 0)))
    n1_high, n1_low = split_two(normalized_one)
    n1_s = dot(pick, n1_high, 1, 0) + dot(pick, n1_low, 1, 0)
    r1_s = jnp.sum(jnp.where(pick > 0, inv_std_one.T, 0.0), axis=1, keepdims=True)
    normed_s = n1_s * gain_one + ln1_bias.astype(f32)
    normed_low_s = dot(pick, normed_low, 1, 0).astype(bf16)
    mixed_s = dot(pick, mixed, 1, 0).astype(bf16)
    emb_s = dot(pick, emb_low, 1, 0).astype(bf16)
    queries_s = jnp.einsum("mw,hwd->hmd", pick, queries, preferred_element_type=f32).astype(bf16)
    hidden_pre_s = dot(normed_low_s, up_weight, 1, 0) + up_bias.astype(f32)
    hidden_s = gelu(hidden_pre_s).astype(bf16)
    ffn_s = dot(hidden_s, down_weight, 1, 0)

    theirs = lax.dynamic_slice_in_dim(ffn_part, (1 - side) * rows_here, rows_here, 0)
    got = pair_swap(jnp.concatenate([theirs, ffn_s], axis=0).astype(bf16)).astype(f32)
    start = side * rows_here
    second = (
        lax.dynamic_slice_in_dim(normed, start, rows_here, 0)
        + (lax.dynamic_slice_in_dim(ffn_part, start, rows_here, 0) + got[:rows_here])
        + down_bias.astype(f32)
    )
    normalized_two, _ = norm_forward(second)
    result = normalized_two * gain_two + ln2_bias.astype(f32)
    n2_s, r2_s = norm_forward(normed_s + (ffn_s + got[rows_here:]) + down_bias.astype(f32))

    grad_second = norm_backward(slot_grad, n2_s, r2_s, gain_two)
    ln2_gain_grad = jnp.sum(slot_grad * n2_s, axis=0)
    ln2_bias_grad = jnp.sum(slot_grad, axis=0)
    dffn = grad_second.astype(bf16)
    down_bias_grad = jnp.sum(dffn, axis=0, dtype=f32)
    down_grad_t = dot(dffn, hidden_s, 0, 0)
    dpre = (dot(dffn, down_weight, 1, 1) * gelu_slope(hidden_pre_s)).astype(bf16)
    up_bias_grad = jnp.sum(dpre, axis=0, dtype=f32)
    up_grad = dot(normed_low_s, dpre, 0, 0)
    dn_part = dot(dpre, up_weight, 1, 1)
    grad_normed = grad_second + (dn_part + pair_swap(dn_part.astype(bf16)).astype(f32))
    grad_first = norm_backward(grad_normed, n1_s, r1_s, gain_one)
    ln1_gain_grad = jnp.sum(grad_normed * n1_s, axis=0)
    ln1_bias_grad = jnp.sum(grad_normed, axis=0)
    dattn = grad_first.astype(bf16)
    out_bias_grad = jnp.sum(dattn, axis=0, dtype=f32)
    out_grad_t = dot(dattn, mixed_s, 0, 0)
    dmixed = by_head(dot(dattn, out_weight, 1, 1).astype(bf16))
    probs = probs_of(queries_s)
    dvalues = jnp.einsum("hqk,hqd->khd", probs.astype(bf16), dmixed, preferred_element_type=f32)
    dprobs = jnp.einsum("hqd,hkd->hqk", dmixed, values, preferred_element_type=f32)
    dscores = (probs * (dprobs - jnp.sum(probs * dprobs, axis=-1, keepdims=True))).astype(bf16)
    dqueries = jnp.einsum("hqk,hkd->qhd", dscores, keys, preferred_element_type=f32) * scale
    dkeys = jnp.einsum("hqk,hqd->khd", dscores, queries_s, preferred_element_type=f32) * scale
    dq = dqueries.reshape(padded_slots, width).astype(bf16)
    dk = dkeys.reshape(words, width).astype(bf16)
    dv = dvalues.reshape(words, width).astype(bf16)
    qv_bias_grad = jnp.stack([jnp.sum(dq, axis=0, dtype=f32), jnp.sum(dv, axis=0, dtype=f32)])
    qkvo_grad = [dot(emb_s, dq, 0, 0), dot(emb_low, dk, 0, 0), dot(emb_low, dv, 0, 0), out_grad_t]
    dq_high, dq_low = split_two(dot(dq, qkv_t[0], 1, 1))
    gf_high, gf_low = split_two(grad_first)
    back = dot(pick, jnp.concatenate([dq_high, gf_high], axis=1), 0, 0) + dot(
        pick, jnp.concatenate([dq_low, gf_low], axis=1), 0, 0
    )
    de_part = back[:, :D] + dot(dk, qkv_t[1], 1, 1) + dot(dv, qkv_t[2], 1, 1)
    encoder_grads = [
        g.astype(bf16).reshape(ndp, D // ndp, -1)
        for g in (up_grad, down_grad_t, jnp.concatenate(qkvo_grad, axis=1))
    ]
    up_mine, down_mine, qkvo_mine, de_other = scatter_blocks(
        encoder_grads, lines, 3, swap=de_part.astype(bf16)
    )
    grad_embedded = back[:, D:] + (de_part + de_other.astype(f32))
    demb = grad_embedded.astype(bf16)

    proj_bias_grad = jnp.sum(demb, axis=0, dtype=f32)
    proj_grad = dot(state_low, demb, 1, 0)
    grad_state = dot(proj_all, demb, 1, 1)
    highway_mine = [None] * layers
    highway_bias_grads = [None] * layers
    for i in reversed(range(layers)):
        state_in, state_full, nonlin, gate = kept[i]
        d_nonlin = (grad_state * (1.0 - gate) * gelu_slope(nonlin)).astype(bf16)
        d_gate = (grad_state * (state_in - gelu(nonlin)) * gate * (1.0 - gate)).astype(bf16)
        d_pre = jnp.stack(
            [d_nonlin.reshape(ndp, per, words), d_gate.reshape(ndp, per, words)], axis=1
        ).reshape(2 * own, words)
        highway_grad = dot(d_pre, state_full, 1, 1).astype(bf16).reshape(ndp, 2 * per, FILTERS)
        highway_bias_grads[i] = jnp.sum(d_pre, axis=1, dtype=f32)
        back_part = dot(highway_all[i], d_pre, 0, 0).reshape(ndp, 2, per, words)
        mine = jnp.where(side == 0, back_part[:, 0], back_part[:, 1]).reshape(own, words)
        other = jnp.where(side == 0, back_part[:, 1], back_part[:, 0]).reshape(own, words)
        ready = [highway_grad]
        if i == layers - 1:
            ready.append(proj_grad.astype(bf16).reshape(ndp, per, D))
        highway_mine[i], *rest, theirs = scatter_blocks(ready, lines, 4 + i, swap=other.astype(bf16))
        if rest:
            proj_mine = rest[0]
        grad_state = grad_state * gate + (mine + theirs.astype(f32))
    grad_pooled = grad_state * gelu_slope(pooled)
    conv_bias_grad = jnp.sum(grad_pooled, axis=1)
    conv_grad, table_grad_t = conv_backward(
        ids, chars, conv_all, lim, pooled_raw, grad_pooled, per, padded_ids
    )
    tap_mask = (tap_shift[None, :] < filter_width[:, None])[:, :taps_used]
    conv_grad = jnp.where(tap_mask, conv_grad[:, :taps_used], 0.0)

    bias_grads = [conv_bias_grad[:, None]]
    for i in range(layers):
        both = highway_bias_grads[i].reshape(ndp, 2, per).transpose(0, 2, 1).reshape(own, 2)
        bias_grads.append(both)
    conv_pack = jnp.concatenate(
        [conv_grad, *bias_grads, jnp.zeros((own, TAPS - taps_used - 1 - 2 * layers), f32)], axis=1
    )
    (conv_mine,) = scatter_blocks([conv_pack.reshape(ndp, per, TAPS)], lines, 4 + layers)
    first = side == 0
    shared = [
        jnp.where(first, g, 0.0)
        for g in (
            proj_bias_grad, out_bias_grad, ln1_gain_grad, ln1_bias_grad, down_bias_grad,
            ln2_gain_grad, ln2_bias_grad,
        )
    ]
    own_side = jnp.concatenate([qv_bias_grad.reshape(-1), up_bias_grad])
    flat = jnp.concatenate(
        [
            table_grad_t.reshape(-1),
            *shared,
            jnp.where(first, own_side, 0.0),
            jnp.where(first, 0.0, own_side),
        ]
    )
    rows_flat = -(-flat.shape[0] // 1024) * 8
    flat = jnp.pad(flat, (0, rows_flat * 128 - flat.shape[0])).reshape(rows_flat, 128)
    flat = total_all(flat, lines, 5 + layers).reshape(-1)
    at = table_grad_t.size
    table_grad_t = flat[:at].reshape(table_grad_t.shape)
    (
        proj_bias_grad, out_bias_grad, ln1_gain_grad, ln1_bias_grad, down_bias_grad, ln2_gain_grad,
        ln2_bias_grad,
    ) = (flat[at + i * D : at + (i + 1) * D] for i in range(7))
    at += 7 * D
    size = own_side.shape[0]
    own_side = jnp.where(first, flat[at : at + size], flat[at + size : at + 2 * size])
    qv_bias_grad = own_side[: 2 * width].reshape(2, width)
    up_bias_grad = own_side[2 * width :]
    conv_bias_mine = conv_mine[:, taps_used]
    highway_bias_mine = [
        conv_mine[:, taps_used + 1 + 2 * i : taps_used + 3 + 2 * i].T for i in range(layers)
    ]
    conv_mine = conv_mine[:, :taps_used]
    qkv_mine = jnp.stack([qkvo_mine[:, i * width : (i + 1) * width] for i in range(3)])
    out_mine = qkvo_mine[:, 3 * width :]
    highway_mine = jnp.stack(highway_mine).reshape(layers, 2, per, FILTERS).transpose(0, 3, 1, 2)
    highway_bias_mine = jnp.stack(highway_bias_mine).reshape(layers, 2, per)
    return (
        result.astype(bf16),
        table_grad_t.T[:ids_count],
        conv_mine.T,
        conv_bias_mine,
        highway_mine,
        highway_bias_mine,
        proj_mine,
        proj_bias_grad,
        qkv_mine.transpose(1, 0, 2),
        qv_bias_grad,
        out_mine.T,
        out_bias_grad,
        ln1_gain_grad,
        ln1_bias_grad,
        up_mine,
        up_bias_grad,
        down_mine.T,
        down_bias_grad,
        ln2_gain_grad,
        ln2_bias_grad,
    )


def solution(mesh):
    placed = (
        P(("dp", "tensor"), None),
        P("dp", None),
        P("dp", None, None),
        P(),
        P(None, ("dp", "tensor")),
        P(("dp", "tensor")),
        P(None, None, None, ("dp", "tensor")),
        P(None, None, ("dp", "tensor")),
        P(("dp", "tensor"), None),
        P(),
        P(None, None, "tensor"),
        P(None, "tensor"),
        P("tensor", None),
        P(),
        P(),
        P(),
        P(None, "tensor"),
        P("tensor"),
        P("tensor", None),
        P(),
        P(),
        P(),
    )
    return jax.shard_map(
        per_device,
        mesh=mesh,
        in_specs=placed,
        out_specs=(
            P(("dp", "tensor"), None),
            P(),
            P(None, ("dp", "tensor")),
            P(("dp", "tensor")),
            P(None, None, None, ("dp", "tensor")),
            P(None, None, ("dp", "tensor")),
            P(("dp", "tensor"), None),
            P(),
            P("dp", None, "tensor"),
            P(None, "tensor"),
            P("tensor", "dp"),
            P(),
            P(),
            P(),
            P("dp", "tensor"),
            P("tensor"),
            P("tensor", "dp"),
            P(),
            P(),
            P(),
        ),
        check_vma=False,
    )
```

time: 2350 us -> 839 us (0.36)
  waiting for transfers between devices: 1170 us -> 51.3 us
  Pallas kernels: 0 us -> 534 us
  blocking collectives: 347 us -> 4.86 us
  matrix products: 302 us -> 105 us
  other arithmetic: 248 us -> 56.9 us
  local copies, waits for them, and re-layouts: 256 us -> 65.1 us
    reduce_scatter x10 -> x0, waiting for transfers between devices: 603 us -> none  [the longest x1 137 us: per_device(): lax.psum_scatter(conv_weight_total, ('dp', 'tensor'), scatter_dimension=1...]
    unnamed x16 -> x0, waiting for transfers between devices: 567 us -> none
    pallas_call x0 -> x9, Pallas kernels: none -> 534 us  [the longest x4 220 us: scatter_blocks(): pl.pallas_call(functools.partial(scatter_kernel, lines, count, pieces, le...]
    dot_general x55 -> x40, matrix products: 302 us -> 96 us  [the longest x34 85.5 us: dot(): lax.dot_general(a, b, (((ca,), (cb,)), ((), ())), preferred_element_type=...]
    all_gather x6 -> x1, blocking collectives: 196 us -> 4.86 us  [per_device(): ids = lax.all_gather(char_ids.T, PAIR, axis=1, tiled=True)]
    reduce_sum x26 -> x14, other arithmetic: 154 us -> 9.37 us  [the longest x2 3.08 us: norm_forward(): centred = summed - jnp.mean(summed, axis=-1, keepdims=True)]
    another operation x8, local copies, waits for them, and re-layouts: 132 us -> 3.1 us  [the longest x4 131 us: highway_backward(): return (grad_state, jnp.stack(weight_grads), jnp.stack(bias_grads))]
    psum x2 -> x0, blocking collectives: 107 us -> none  [the longest x1 65.4 us: per_device(): qv_bias_grad, up_bias_grad = lax.psum((qv_bias_grad, up_bias_grad), 'dp')]
  transfers between devices with their start and end apart: 14 -> 5, of which waited for: 11 -> 4; matrix products, arithmetic and copies ran while one was open for 28% -> 5% of each run, Pallas kernels for 0% -> 0%
where the time goes in v1:
time: 839 us; the launch traced here: 825 us
  Pallas kernels  534 us (64%)
  matrix products  105 us (13%)
  local copies, waits for them, and re-layouts  65.1 us (8%)
  other arithmetic  56.9 us (7%)
  waiting for transfers between devices  51.3 us (6%)
    pallas_call x4, Pallas kernels, scatter_blocks(): pl.pallas_call(functools.partial(scatter_kernel, lines, count, pieces, le...  220 us
    pallas_call x2, Pallas kernels, gather_blocks(): pl.pallas_call(functools.partial(gather_kernel, lines, count, len(swaps))...  117 us
    pallas_call x1, Pallas kernels, conv_forward(): pl.pallas_call(functools.partial(conv_forward_kernel, limits), out_shape=...  108 us
    dot_general x34, matrix products, dot(): lax.dot_general(a, b, (((ca,), (cb,)), ((), ())), preferred_element_type=...  85.5 us
    pallas_call x1, Pallas kernels, conv_backward(): pl.pallas_call(functools.partial(conv_backward_kernel, limits), out_shape...  69.9 us
    ppermute x5, waiting for transfers between devices, pair_swap(): return lax.ppermute(x, PAIR, [(0, 1), (1, 0)])  51.3 us
    dot_general x3, local copies, waits for them, and re-layouts, dot(): lax.dot_general(a, b, (((ca,), (cb,)), ((), ())), preferred_element_type=...  26.3 us
    pallas_call x1, Pallas kernels, total_all(): pl.pallas_call(functools.partial(total_kernel, lines), out_shape=jax.Shap...  19.1 us
  transfers between devices with their start and end apart: 5, of which 4 were waited for; matrix products, arithmetic and copies ran while one was open for 5% of the time, Pallas kernels for 0%

profile of v1, /device:TPU:0, one launch (start us, length us, event | category | flops | bytes accessed | tf_op | source)
XLA Modules:
  0.0 825.4 jit_solution(4790091060216280489)
XLA Ops:
  6.2 57.8 %shard_map.365 = (f32[4,2,2,64,128]{4,3,2,1,0:T(8,128)}, bf16[4,2,2,128,2048]{4,3,2,1,0:T(8,128)(2,1)}) custom-call(f32[64,128]{1,0:T(8,128)} %maximum_maximum_fusion.refs_0_, bf16[128,2048]{1,0:T(8,128)(2,1)} %bitcast.441), custom_call_target="tpu_custom_call" | custom-call | tf_op jit(solution)/shard_map/pallas_call | solution.py:245
  69.1 4.9 all_gather.3.ids_ref
  75.5 108.2 %shard_map.366 = (f32[1024,512]{1,0:T(8,128)S(1)}, bf16[912,512]{1,0:T(8,128)(2,1)S(1)}) custom-call(s32[50,512]{1,0:T(8,128)S(1)} %all_gather.3.ids_ref, bf16[16,384]{1,0:T(8,128)(2,1)S(1)} %pad.16.table_ref, bf16[1024,128]{1,0:T(8,128)(2,1)S(1)} %copy.120.weight_ref, s32[1024,128]{1,0:T(8,128)S(1)} %broadcast_in_dim.40.lim_ref), custom_call_target="tpu_custom_call" | custom-call | flops 14000000000 | bytes 8388608 | tf_op jit(solution)/shard_map/pallas_call | solution.py:581
  183.7 6.1 fusion.219
  189.9 58.9 %shard_map.367 = (bf16[4,2,2,128,2048]{4,3,2,1,0:T(8,128)(2,1)}, bf16[4,2,2,64,768]{4,3,2,1,0:T(8,128)(2,1)}, bf16[1024,512]{1,0:T(8,128)(2,1)}) custom-call(bf16[128,2048]{1,0:T(8,128)(2,1)} %bitcast.438, bf16[64,768]{1,0:T(8,128)(2,1)} %refs_1_.1, bf16[1024,512]{1,0:T(8,128)(2,1)} %get-tuple-element.93.refs_2_), custom_call_target="tpu_custom_call" | custom-call | tf_op jit(solution)/shard_map/pallas_call | solution.py:245
  251.9 6.9 broadcast_add_fusion.1
  260.4 6.0 fusion.216
  269.0 22.8 %collective-permute-done = bf16[1024,512]{1,0:T(8,128)(2,1)} collective-permute-done((bf16[1024,512]{1,0:T(8,128)(2,1)S(1)}, bf16[1024,512]{1,0:T(8,128)(2,1)}, u32[]{:S(2)}, u32[]{:S(2)}) %collective-permute-start) | collective-permute-done | bytes 1048608 | tf_op jit(solution)/shard_map/ppermute | solution.py:63
  294.9 6.9 broadcast_add_fusion
  303.4 5.9 fusion.54
  312.9 17.3 %collective-permute-done.1 = bf16[512,768]{1,0:T(8,128)(2,1)S(1)} collective-permute-done((bf16[512,768]{1,0:T(8,128)(2,1)S(1)}, bf16[512,768]{1,0:T(8,128)(2,1)S(1)}, u32[]{:S(2)}, u32[]{:S(2)}) %collective-permute-start.1) | collective-permute-done | bytes 786464 | tf_op jit(solution)/shard_map/ppermute | solution.py:63
  333.6 5.9 fusion.227
  339.4 3.5 fusion.100
  350.3 12.3 %copy.132 = bf16[2048,2048]{1,0:T(8,128)(2,1)} copy(bf16[2048,2048]{0,1:T(8,128)(2,1)} %bitcast.409) | data formatting | bytes 16777216 | tf_op jit(solution)/shard_map/dot_general | solution.py:46
  362.6 12.5 %copy.134 = bf16[2048,2048]{1,0:T(8,128)(2,1)} copy(bf16[2048,2048]{0,1:T(8,128)(2,1)} %bitcast.407) | data formatting | bytes 16777216 | tf_op jit(solution)/shard_map/dot_general | solution.py:46
  380.0 3.0 fusion.231
  390.4 12.5 %fusion.95 = f32[512,768]{1,0:T(8,128)} fusion(bf16[1536,768]{1,0:T(8,128)(2,1)} %param.40, bf16[768,1536]{1,0:T(8,128)(2,1)S(1)} %copy-done, f32[1536]{0:T(1024)S(1)} %copy-done.87, f32[512,768]{1,0:T(8,128)} %copy-done.36), kind=kOutput, calls=%fused_computation.184 | convolution fusion | flops 2468216832 | bytes 7870464 | tf_op jit(solution)/shard_map/dot_general | solution.py:46
  411.9 8.0 collective-permute-done.3
  431.8 3.1 collective-permute-done.4
  436.4 3.2 convert_reduce_fusion.1
  454.1 59.5 %shard_map.368 = (bf16[4,2,48,1536]{3,2,1,0:T(8,128)(2,1)}, bf16[4,2,48,1536]{3,2,1,0:T(8,128)(2,1)}, bf16[4,2,48,1536]{3,2,1,0:T(8,128)(2,1)}, bf16[4,48,1536]{...) custom-call(bf16[4,2,2,48,1536]{4,3,2,1,0:T(8,128)(2,1)} %bitcast.39, ...), custom_call_target="tpu_custom_call" | custom-call | tf_op jit(solution)/shard_map/pallas_call | solution.py:476
  518.1 3.0 fusion.29
  521.7 4.6 fusion.233
  528.4 6.9 convolution_convert_fusion.1
  535.3 79.6 %shard_map.369 = (bf16[4,2,128,2048]{3,2,1,0:T(8,128)(2,1)}, bf16[4,2,64,768]{3,2,1,0:T(8,128)(2,1)}, bf16[4,128,2048]{2,1,0:T(8,128)(2,1)}, bf16[4,64,768]{2,1,...) custom-call(bf16[4,2,2,128,2048]{4,3,2,1,0:T(8,128)(2,1)} %bitcast.4, ...), custom_call_target="tpu_custom_call" | custom-call | tf_op jit(solution)/shard_map/pallas_call | solution.py:476
  614.9 3.3 fusion.35
  620.6 4.7 fusion.234
  627.1 6.9 convolution_convert_fusion
  634.0 64.4 %shard_map.370 = (bf16[4,2,128,2048]{3,2,1,0:T(8,128)(2,1)}, bf16[4,128,2048]{2,1,0:T(8,128)(2,1)}, bf16[4,128,2048]{2,1,0:T(8,128)(2,1)}, f32[128,2048]{1,0:T(8,128)S(1)}, bf16[1024,512]{1,0:T(8,128)(2,1)S(1)}) custom-call(bf16[4,2,2,128,2048]{4,3,2,1,0:T(8,128)(2,1)} %bitcast.399, bf16[1024,512]{1,0:T(8,128)(2,1)S(1)} %bitcast.392), custom_call_target="tpu_custom_call" | custom-call | tf_op jit(solution)/shard_map/pallas_call | solution.py:476
  701.5 69.9 %shard_map.371 = (f32[1024,128]{1,0:T(8,128)S(1)}, f32[16,384]{1,0:T(8,128)S(1)}) custom-call(s32[50,512]{1,0:T(8,128)S(1)} %copy-done.19, bf16[912,512]{1,0:T(8,128)(2,1)S(1)} %copy-done.21, bf16[1024,128]{1,0:T(8,128)(2,1)S(1)} %copy-done.14, bf16[128,1024]{1,0:T(8,128)(2,1)S(1)} %copy-done.15, s32[1024,128]{1,0:T(8,128)S(1)} %copy-done.6, ...), custom_call_target="tpu_custom_call" | custom-call | flops 41999998976 | bytes 8388608 | tf_op jit(solution)/shard_map/pallas_call | solution.py:648
  773.5 16.9 %shard_map.373 = (bf16[4,2,64,128]{3,2,1,0:T(8,128)(2,1)}, bf16[4,64,128]{2,1,0:T(8,128)(2,1)}, bf16[4,64,128]{2,1,0:T(8,128)(2,1)}, f32[64,128]{1,0:T(8,128)S(1)}) custom-call(bf16[4,2,2,64,128]{4,3,2,1,0:T(8,128)(2,1)S(1)} %concatenate.61.refs_0_), custom_call_target="tpu_custom_call" | custom-call | tf_op jit(solution)/shard_map/pallas_call | solution.py:476
  792.9 19.1 %shard_map.372 = f32[128,128]{1,0:T(8,128)} custom-call(f32[128,128]{1,0:T(8,128)} %pad_bitcast_fusion.x_ref), custom_call_target="tpu_custom_call" | custom-call | tf_op jit(solution)/shard_map/pallas_call | solution.py:515
  (394 shorter events, 118.3 us)
Async XLA Ops:
  0.7 387.6 %copy-start = (bf16[768,1536]{1,0:T(8,128)(2,1)S(1)}, bf16[768,1536]{1,0:T(8,128)(2,1)}, u32[]{:S(2)}) copy-start(bf16[768,1536]{1,0:T(8,128)(2,1)} %param.38) | copy-start | bytes 7077892
  0.7 73.3 %copy-start.104 = (pred[128]{0:T(512)(128)(4,1)}, pred[128]{0:T(512)(128)(4,1)S(1)}, u32[]{:S(2)}) copy-start(pred[128]{0:T(512)(128)(4,1)S(1)} %iota_compare_fusion.9) | copy-start | bytes 388
  0.7 345.7 %copy-start.91 = (s32[128]{0:T(128)}, s32[128]{0:T(128)S(1)}, u32[]{:S(2)}) copy-start(s32[128]{0:T(128)S(1)} %and_select_fusion) | copy-start | bytes 1540
  5.4 63.7 %copy-start.78 = (s32[256,50]{0,1:T(8,128)S(1)}, s32[256,50]{0,1:T(8,128)}, u32[]{:S(2)}) copy-start(s32[256,50]{0,1:T(8,128)} %param.22) | copy-start | bytes 153604
  66.7 117.0 %copy-start.80 = (f32[1024]{0:T(1024)}, f32[1024]{0:T(1024)S(1)}, u32[]{:S(2)}) copy-start(f32[1024]{0:T(1024)S(1)} %slice_reduce_fusion) | copy-start | bytes 12292
  74.0 109.7 %copy-start.18 = (s32[50,512]{1,0:T(8,128)}, s32[50,512]{1,0:T(8,128)S(1)}, u32[]{:S(2)}) copy-start(s32[50,512]{1,0:T(8,128)S(1)} %all_gather.3.ids_ref) | copy-start | bytes 307204
  74.4 109.3 %copy-start.13 = (bf16[1024,128]{1,0:T(8,128)(2,1)}, bf16[1024,128]{1,0:T(8,128)(2,1)S(1)}, u32[]{:S(2)}) copy-start(bf16[1024,128]{1,0:T(8,128)(2,1)S(1)} %copy.120.weight_ref) | copy-start | bytes 786436
  75.5 108.2 %copy-start.5 = (s32[1024,128]{1,0:T(8,128)}, s32[1024,128]{1,0:T(8,128)S(1)}, u32[]{:S(2)}) copy-start(s32[1024,128]{1,0:T(8,128)S(1)} %broadcast_in_dim.40.lim_ref) | copy-start | bytes 1572868
  189.9 58.9 %copy-start.39 = (bf16[1024,512]{1,0:T(8,128)(2,1)S(1)}, bf16[1024,512]{1,0:T(8,128)(2,1)}, u32[]{:S(2)}) copy-start(bf16[1024,512]{1,0:T(8,128)(2,1)} %get-tuple-element.93.refs_2_) | copy-start | bytes 3145732
  266.4 25.3 %collective-permute-start = (bf16[1024,512]{1,0:T(8,128)(2,1)S(1)}, bf16[1024,512]{1,0:T(8,128)(2,1)}, u32[]{:S(2)}, u32[]{:S(2)}) collective-permute-start(bf16[1024,512]{1,0:T(8,128)(2,1)S(1)} %get-tuple-element.90), channel_id=1, source_target_pairs={{0,1},{1,0},{2,3},{3,2},{4,5},{5,4},{6,7},{7,6},{8,9},{9,8},{10,11... | collective-permute-start | bytes 3145736 | tf_op jit(solution)/shard_map/ppermute | solution.py:63
  311.3 20.4 %copy-start.44 = (f32[512,768]{1,0:T(8,128)}, f32[512,768]{1,0:T(8,128)S(1)}, u32[]{:S(2)}) copy-start(f32[512,768]{1,0:T(8,128)S(1)} %get-tuple-element.129) | copy-start | bytes 4718596
  311.3 19.1 %copy-start.58 = (bf16[768,3,384]{2,0,1:T(8,128)(2,1)S(1)}, bf16[768,3,384]{2,0,1:T(8,128)(2,1)}, u32[]{:S(2)}) copy-start(bf16[768,3,384]{2,0,1:T(8,128)(2,1)} %param.32) | copy-start | bytes 5308420
  311.4 18.9 %collective-permute-start.1 = (bf16[512,768]{1,0:T(8,128)(2,1)S(1)}, bf16[512,768]{1,0:T(8,128)(2,1)S(1)}, u32[]{:S(2)}, u32[]{:S(2)}) collective-permute-start(bf16[512,768]{1,0:T(8,128)(2,1)S(1)} %get-tuple-element.128), channel_id=1, source_target_pairs={{0,1},{1,0},{2,3},{3,2},{4,5},{5,4},{6,7},{7,6},{8,9},{9,8},{10,11... | collective-permute-start | bytes 2359304 | tf_op jit(solution)/shard_map/ppermute | solution.py:63
  312.7 19.0 %copy-start.82 = (f32[768]{0:T(1024)}, f32[768]{0:T(1024)S(1)}, u32[]{:S(2)}) copy-start(f32[768]{0:T(1024)S(1)} %convert_element_type.380) | copy-start | bytes 9220
  333.5 46.5 %copy-start.64 = (bf16[512,384]{0,1:T(8,128)(2,1)}, bf16[512,384]{0,1:T(8,128)(2,1)S(1)}, u32[]{:S(2)}) copy-start(bf16[512,384]{0,1:T(8,128)(2,1)S(1)} %fusion.98) | copy-start | bytes 1179652
  345.1 37.9 %collective-permute-start.2 = (bf16[512,768]{1,0:T(8,128)(2,1)}, bf16[512,768]{1,0:T(8,128)(2,1)}, u32[]{:S(2)}, u32[]{:S(2)}) collective-permute-start(bf16[512,768]{1,0:T(8,128)(2,1)} %get-tuple-element.132), channel_id=1, source_target_pairs={{0,1},{1,0},{2,3},{3,2},{4,5},{5,4},{6,7},{7,6},{8,9},{9,8},{10,11... | collective-permute-start | bytes 2359304 | tf_op jit(solution)/shard_map/ppermute | solution.py:63
  362.6 13.1 %copy-start.52 = (bf16[1024,128]{0,1:T(8,128)(2,1)S(1)}, bf16[1024,128]{0,1:T(8,128)(2,1)}, u32[]{:S(2)}) copy-start(bf16[1024,128]{0,1:T(8,128)(2,1)} %copy-done.51) | copy-start | bytes 786436
  362.6 13.1 %copy-start.92 = (s32[128]{0:T(128)S(1)}, s32[128]{0:T(128)}, u32[]{:S(2)}) copy-start(s32[128]{0:T(128)} %copy-done.91) | copy-start | bytes 1540
  362.6 13.1 %copy-start.105 = (pred[128]{0:T(512)(128)(4,1)S(1)}, pred[128]{0:T(512)(128)(4,1)}, u32[]{:S(2)}) copy-start(pred[128]{0:T(512)(128)(4,1)} %copy-done.104) | copy-start | bytes 388
  407.9 12.1 %collective-permute-start.3 = (bf16[336,768]{1,0:T(8,128)(2,1)}, bf16[336,768]{1,0:T(8,128)(2,1)}, u32[]{:S(2)}, u32[]{:S(2)}) collective-permute-start(bf16[336,768]{1,0:T(8,128)(2,1)} %pad_maximum_fusion.5), channel_id=1, source_target_pairs={{0,1},{1,0},{2,3},{3,2},{4,5},{5,4},{6,7},{7,6},{8,9},{9,8},{10,11... | collective-permute-start | bytes 1548296 | tf_op jit(solution)/shard_map/ppermute | solution.py:63
  409.9 25.3 %copy-start.89 = (f32[80]{0:T(128)}, f32[80]{0:T(128)S(1)}, u32[]{:S(2)}) copy-start(f32[80]{0:T(128)S(1)} %select_reduce_fusion) | copy-start | bytes 964
  430.0 4.9 collective-permute-start.4
  454.1 60.4 %copy-start.67 = (bf16[1024,512]{1,0:T(8,128)(2,1)S(1)}, bf16[1024,512]{1,0:T(8,128)(2,1)}, u32[]{:S(2)}) copy-start(bf16[1024,512]{1,0:T(8,128)(2,1)} %copy-done.66) | copy-start | bytes 3145732
  454.1 62.5 %copy-start.60 = (bf16[4,2,2,64,768]{4,3,2,1,0:T(8,128)(2,1)S(1)}, bf16[4,2,2,64,768]{4,3,2,1,0:T(8,128)(2,1)}, u32[]{:S(2)}) copy-start(bf16[4,2,2,64,768]{4,3,2,1,0:T(8,128)(2,1)} %get-tuple-element.44) | copy-start | bytes 4718596
  535.3 79.6 %copy-start.23 = (f32[16,1,64,512]{3,2,1,0:T(8,128)S(1)}, f32[16,1,64,512]{3,2,1,0:T(8,128)}, u32[]{:S(2)}) copy-start(f32[16,1,64,512]{3,2,1,0:T(8,128)} %copy-done.22) | copy-start | bytes 6291460
  535.3 79.6 %copy-start.29 = (f32[16,1,64,512]{3,2,1,0:T(8,128)S(1)}, f32[16,1,64,512]{3,2,1,0:T(8,128)}, u32[]{:S(2)}) copy-start(f32[16,1,64,512]{3,2,1,0:T(8,128)} %copy-done.28) | copy-start | bytes 6291460
  634.0 64.4 %copy-start.3 = (f32[1024,512]{1,0:T(8,128)S(1)}, f32[1024,512]{1,0:T(8,128)}, u32[]{:S(2)}) copy-start(f32[1024,512]{1,0:T(8,128)} %copy-done.2) | copy-start | bytes 6291460
  634.0 64.4 %copy-start.81 = (f32[1024]{0:T(1024)S(1)}, f32[1024]{0:T(1024)}, u32[]{:S(2)}) copy-start(f32[1024]{0:T(1024)} %copy-done.80) | copy-start | bytes 12292
  701.5 70.1 %copy-start.74 = (pred[1024,128]{0,1:T(8,128)(4,1)S(1)}, pred[1024,128]{0,1:T(8,128)(4,1)}, u32[]{:S(2)}) copy-start(pred[1024,128]{0,1:T(8,128)(4,1)} %broadcast_compare_fusion) | copy-start | bytes 393220
  771.6 20.3 %copy-start.94 = (f32[6,64]{1,0:T(8,128)S(1)}, f32[6,64]{1,0:T(8,128)}, u32[]{:S(2)}) copy-start(f32[6,64]{1,0:T(8,128)} %get-tuple-element.150) | copy-start | bytes 4612
  771.6 20.4 %copy-start.85 = (f32[768]{0:T(1024)S(1)}, f32[768]{0:T(1024)}, u32[]{:S(2)}) copy-start(f32[768]{0:T(1024)} %get-tuple-element.73) | copy-start | bytes 9220
  771.9 45.5 %copy-start.12 = (f32[48,1536]{1,0:T(8,128)S(1)}, f32[48,1536]{1,0:T(8,128)}, u32[]{:S(2)}) copy-start(f32[48,1536]{1,0:T(8,128)} %copy-done.11) | copy-start | bytes 884740
  (86 other events, 334.5 us)

commit v2 on v1

--- a/solution.py
+++ b/solution.py
@@ -29,13 +29,12 @@
 
 
 def gelu(x):
-    return jax.nn.gelu(x, approximate=False)
-
-
-def gelu_slope(x):
-    return 0.5 * (1.0 + lax.erf(x * (1.0 / math.sqrt(2.0)))) + x * jnp.exp(-0.5 * x * x) * (
-        1.0 / math.sqrt(2.0 * math.pi)
-    )
+    return 0.5 * x * (1.0 + lax.erf(x * (1.0 / math.sqrt(2.0))))
+
+
+def gelu_both(x):
+    share = 0.5 * (1.0 + lax.erf(x * (1.0 / math.sqrt(2.0))))
+    return x * share, share + x * jnp.exp(-0.5 * x * x) * (1.0 / math.sqrt(2.0 * math.pi))
 
 
 def width_of(channel):
@@ -389,16 +388,16 @@
 
         lax.fori_loop(0, size // 16, each, 0)
 
-    def steps(self):
-        count = len(self.pieces)
+    def order(self, count):
         work = []
-        for k in range(count + 4):
+        lead = self.sums.shape[0] - 1
+        for k in range(count + lead + 2):
             if k < count:
-                work.append(functools.partial(self.add_core, k))
-            if 0 <= k - 2 < count:
-                work.append(functools.partial(self.add_row, k - 2))
-            if 0 <= k - 4 < count:
-                work.append(functools.partial(self.add_line, k - 4))
+                work.append(("add_core", k))
+            if 0 <= k - lead < count:
+                work.append(("add_row", k - lead))
+            if 0 <= k - lead - 2 < count:
+                work.append(("add_line", k - lead - 2))
         return work
 
     def finish(self):
@@ -421,36 +420,14 @@
         width = max(a.shape[-1] for a in arrays)
         dma = pltpu.SemaphoreType.DMA
         count = len(pieces)
+        slots = 4 if lines <= 8 else 2
         bufs = [
             pltpu.VMEM((lines, 2, rows, width), bf16), pltpu.VMEM((lines, 2, rows, width), bf16),
-            pltpu.VMEM((3, 2, lines, rows, width), bf16), pltpu.VMEM((lines, rows, width), bf16),
-            pltpu.VMEM((2, lines, rows, width), bf16), pltpu.VMEM((lines, rows, width), bf16),
+            pltpu.VMEM((slots, 2, lines, rows, width), bf16), pltpu.VMEM((lines, rows, width), bf16),
+            pltpu.VMEM((slots // 2, lines, rows, width), bf16), pltpu.VMEM((lines, rows, width), bf16),
         ]
         sems = [dma((count,))] * 4 + [dma((count, lines))] * 2 + [dma((5,))]
         return land, outs, bufs, sems
-
-
-def scatter_kernel(lines, count, pieces, swap, *refs):
-    arrays, refs = refs[:count], refs[count:]
-    swap_in, refs = refs[:swap], refs[swap:]
-    land, refs = refs[: 3 * count], refs[3 * count :]
-    outs, refs = refs[:count], refs[count:]
-    swap_out, refs = refs[:swap], refs[swap:]
-    place = Place(lines)
-    scatter = Scatter(
-        place, arrays, land[:count], land[count : 2 * count], land[2 * count :], outs, pieces,
-        refs[:6], refs[6:13],
-    )
-    meet(neighbours(place, bool(swap)))
-    if swap:
-        copy = send(swap_in[0], swap_out[0], refs[13:15], place.partner)
-    for k in range(len(pieces)):
-        scatter.begin(k)
-    for step in scatter.steps():
-        step()
-    scatter.finish()
-    if swap:
-        copy.wait()
 
 
 def cut(arrays, most):
@@ -462,199 +439,556 @@
     return pieces
 
 
-def scatter_blocks(arrays, lines, ident, most=48, swap=None):
-    whole = []
-    for a in arrays:
-        rows = -(-a.shape[1] // 16) * 16
-        a = jnp.pad(a.astype(bf16), ((0, 0), (0, rows - a.shape[1]), (0, 0)))
-        whole.append(a.reshape((lines, 2, 2) + a.shape[1:]))
-    pieces = cut(whole, most)
-    land, outs, bufs, sems = Scatter.shapes(whole, pieces, lines)
-    swaps = [] if swap is None else [swap]
-    dma = pltpu.SemaphoreType.DMA
-    count = len(arrays)
-    result = pl.pallas_call(
-        functools.partial(scatter_kernel, lines, count, pieces, len(swaps)),
-        out_shape=tuple(land + outs + [jax.ShapeDtypeStruct(s.shape, s.dtype) for s in swaps]),
-        in_specs=[ANYWHERE] * (count + len(swaps)),
-        out_specs=tuple(
-            [ANYWHERE] * len(land)
-            + [pl.BlockSpec(memory_space=pltpu.VMEM)] * count
-            + [ANYWHERE] * len(swaps)
-        ),
-        scratch_shapes=bufs + sems + [dma, dma] * len(swaps),
-        compiler_params=pltpu.CompilerParams(
-            collective_id=ident, has_side_effects=True, vmem_limit_bytes=48 << 20
-        ),
-    )(*whole, *swaps)
-    own = [r[: a.shape[1]] for r, a in zip(result[3 * count : 4 * count], arrays)]
-    return own + list(result[4 * count :])
-
-
-def total_kernel(lines, x_ref, o_ref, inbox, send_sems, recv_sems):
-    place = Place(lines)
-    partners = [place.sibling, place.across]
-    span = 1
-    while span < lines:
-        low = lax.rem(place.line // span, 2)
-        partners.append(place.on_line(place.line + span - 2 * span * low))
-        span *= 2
-    partners.append(place.partner)
-    meet(partners)
-    o_ref[...] = x_ref[...]
-    for i, device in enumerate(partners):
-        copy = send(o_ref, inbox.at[i], (send_sems.at[i], recv_sems.at[i]), device)
-        copy.wait()
-        o_ref[...] = o_ref[...] + inbox[i]
-
-
-def total_all(x, lines, ident):
-    count = 3 + (lines - 1).bit_length()
-    dma = pltpu.SemaphoreType.DMA
-    vmem = pl.BlockSpec(memory_space=pltpu.VMEM)
-    return pl.pallas_call(
-        functools.partial(total_kernel, lines),
-        out_shape=jax.ShapeDtypeStruct(x.shape, x.dtype),
-        in_specs=[vmem],
-        out_specs=vmem,
-        scratch_shapes=[pltpu.VMEM((count,) + x.shape, x.dtype), dma((count,)), dma((count,))],
-        compiler_params=pltpu.CompilerParams(collective_id=ident, has_side_effects=True),
-    )(x)
-
-
 def onehot_chars(ids_row, count):
     return jnp.where(
         lax.broadcasted_iota(jnp.int32, (count, ids_row.shape[1]), 0) == ids_row, 1.0, 0.0
     ).astype(bf16)
 
 
-def conv_forward_kernel(limits, ids_ref, table_ref, weight_ref, lim_ref, pooled_ref, chars_ref, conv_ref):
-    words = ids_ref.shape[1]
-    count = table_ref.shape[1]
+class Pooling:
+    group = 32
+
+    def __init__(self, limits, chars, weight, lim, pooled, bufs):
+        self.limits, self.chars, self.weight, self.lim = limits, chars, weight, lim
+        self.pooled, self.bufs = pooled, bufs
+        self.halves = chars.shape[1] // FBLOCK
+        self.units = [(b, h) for b in range(len(limits)) for h in range(self.halves)]
+
+    def convolve(self, u, p):
+        block, half = self.units[u]
+        rows = pl.ds(pl.multiple_of(p * CHAR_DIM, CHAR_DIM), TAPS)
+        taps = self.chars[rows, pl.ds(half * FBLOCK, FBLOCK)]
+        self.bufs[u % 2][p] = dot(self.weight[pl.ds(block * FBLOCK, FBLOCK), :], taps, 1, 0)
+
+    def pool(self, u, g):
+        block, half = self.units[u]
+        full, some = self.limits[block]
+        buf, size = self.bufs[u % 2], self.group
+        here = pl.ds(pl.multiple_of(g * size, size), size)
+        there = pl.ds(pl.multiple_of(block * FBLOCK + g * size, size), size)
+        lim = self.lim[there, :] if some > full else None
+
+        def entry(p):
+            value = buf[p, here, :]
+            return value if p < full else jnp.where(lim[:, :1] >= p, value, big_negative)
+
+        top = entry(0)
+        for p in range(1, some):
+            top = jnp.maximum(top, entry(p))
+        total = jnp.exp(entry(0) - top)
+        for p in range(1, some):
+            total = total + jnp.exp(entry(p) - top)
+        self.pooled[there, pl.ds(half * FBLOCK, FBLOCK)] = top + jnp.log(total)
+
+    def step(self, u):
+        count = FBLOCK // self.group
+        todo = self.limits[self.units[u][0]][1] if u < len(self.units) else 0
+        each = -(-todo // count)
+
+        def body(g, carry):
+            for i in range(each):
+                self.convolve(u, jnp.minimum(g * each + i, todo - 1))
+            if u:
+                self.pool(u - 1, g)
+            return carry
+
+        lax.fori_loop(0, count, body, 0)
+
+
+def embed_kernel(
+    lines, limits, ids_ref, table_ref, lim_ref, packed_ref, highway_ref,
+    packed_all, highway_all, ids_all, chars_ref, weight_ref, pooled_ref, state_ref, low_ref, other_ref,
+    buf_a, buf_b, packed_vmem, ids_s, ids_r, load, state_s, state_r, *sems,
+):
+    place = Place(lines)
+    half = highway_ref.shape[0] // 2
+    gather = Gather(
+        place,
+        [packed_ref] + [highway_ref.at[pl.ds(i * half, half)] for i in range(2)],
+        [packed_all] + [highway_all.at[:, :, :, pl.ds(i * half, half)] for i in range(2)],
+        sems,
+    )
+    meet(neighbours(place, True))
+    gather.begin(0)
+    ids_copy = send(ids_ref, ids_all.at[place.side], (ids_s, ids_r), place.partner)
+    own_copy = pltpu.make_async_copy(ids_ref, ids_all.at[place.side], load)
+    own_copy.start()
+    gather.begin(1)
+    gather.begin(2)
+    own_copy.wait()
+    ids_copy.wait()
+    count = ids_ref.shape[0]
 
     def embed(c, carry):
-        hot = onehot_chars(ids_ref[pl.ds(c, 1), :], count)
-        vec = dot(table_ref[...], hot, 1, 0)
-        chars_ref[pl.ds(pl.multiple_of(c * CHAR_DIM, CHAR_DIM), CHAR_DIM), :] = vec.astype(bf16)
+        for i in range(5):
+            row = pl.ds(c * 5 + i, 1)
+            ids = jnp.concatenate([ids_all[0, row, :], ids_all[1, row, :]], axis=1)
+            hot = onehot_chars(ids, table_ref.shape[1])
+            rows = pl.ds(pl.multiple_of((c * 5 + i) * CHAR_DIM, CHAR_DIM), CHAR_DIM)
+            chars_ref[rows, :] = dot(table_ref[...], hot, 1, 0).astype(bf16)
         return carry
 
-    lax.fori_loop(0, CHARS, embed, 0)
+    lax.fori_loop(0, count // 5, embed, 0)
+    words = chars_ref.shape[1]
     chars_ref[CHARS * CHAR_DIM :, :] = jnp.zeros((VROWS - CHARS * CHAR_DIM, words), bf16)
-
-    for block, (full, some) in enumerate(limits):
-        rows = pl.ds(block * FBLOCK, FBLOCK)
-        for half in range(words // FBLOCK):
-            lanes = pl.ds(half * FBLOCK, FBLOCK)
-
-            def convolve(p, carry):
-                taps = chars_ref[pl.ds(pl.multiple_of(p * CHAR_DIM, CHAR_DIM), TAPS), lanes]
-                conv_ref[p] = dot(weight_ref[rows, :], taps, 1, 0)
+    for r in range(1, lines):
+        gather.turn(0, r)
+    gather.finish(0)
+    copy = pltpu.make_async_copy(packed_all, packed_vmem, load)
+    copy.start()
+    copy.wait()
+    rows = weight_ref.shape[0]
+    packed = packed_vmem[...].reshape(rows, TAPS)
+    shift = lax.broadcasted_iota(jnp.int32, (rows, TAPS), 1)
+    keep = (shift < (CHARS - lim_ref[...]) * CHAR_DIM) & (shift < MAX_WIDTH * CHAR_DIM)
+    weight_ref[...] = jnp.where(keep, packed, 0.0).astype(bf16)
+    gather.turn(1, 1)
+    gather.turn(2, 1)
+
+    pooling = Pooling(limits, chars_ref, weight_ref, lim_ref, pooled_ref, (buf_a, buf_b))
+    steps = len(pooling.units) + 1
+    copies = []
+    due = {max(1, (steps * r) // lines): r for r in range(2, lines)} if lines <= steps else {}
+    for u in range(steps):
+        pooling.step(u)
+        done = u - 1
+        if done >= 0 and done % pooling.halves == pooling.halves - 1:
+            block = done // pooling.halves
+            span = pl.ds(block * FBLOCK, FBLOCK)
+            bias = packed_vmem[...].reshape(rows, TAPS)[block * FBLOCK : (block + 1) * FBLOCK, 112:113]
+            state = gelu(pooled_ref[span, :] + bias)
+            state_ref[span, :] = state
+            low_ref[span, :] = state.astype(bf16)
+            copies.append(
+                send(
+                    low_ref.at[span], other_ref.at[span], (state_s.at[block], state_r.at[block]),
+                    place.partner,
+                )
+            )
+        if u in due:
+            for k in (1, 2):
+                gather.turn(k, due[u])
+    for r in range(2, lines):
+        if r not in due.values():
+            for k in (1, 2):
+                gather.turn(k, r)
+    for k in (1, 2):
+        gather.finish(k)
+    for copy in copies:
+        copy.wait()
+
+
+def embed_words(ids, table, lim, packed, highway, lines, per, ident):
+    own = lim.shape[0]
+    words = 2 * ids.shape[1]
+    limits = tuple(block_limits(per, s, s + FBLOCK) for s in range(0, own, FBLOCK))
+    dma = pltpu.SemaphoreType.DMA
+    vmem = pl.BlockSpec(memory_space=pltpu.VMEM)
+    blocks = len(limits)
+    shape = jax.ShapeDtypeStruct
+    return pl.pallas_call(
+        functools.partial(embed_kernel, lines, limits),
+        out_shape=(
+            shape((lines, 2, 2) + packed.shape, f32),
+            shape((lines, 2, 2) + highway.shape, bf16),
+            shape((2,) + ids.shape, jnp.int32),
+            shape((VROWS, words), bf16),
+            shape((own, TAPS), bf16),
+            shape((own, words), f32),
+            shape((own, words), f32),
+            shape((own, words), bf16),
+            shape((own, words), bf16),
+        ),
+        in_specs=[vmem, vmem, vmem, ANYWHERE, ANYWHERE],
+        out_specs=(ANYWHERE, ANYWHERE, vmem, vmem, vmem, vmem, vmem, vmem, ANYWHERE),
+        scratch_shapes=[
+            pltpu.VMEM((CHARS, FBLOCK, FBLOCK), f32), pltpu.VMEM((CHARS, FBLOCK, FBLOCK), f32),
+            pltpu.VMEM((lines, 2, 2) + packed.shape, f32), dma, dma, dma, dma((blocks,)), dma((blocks,)),
+            *Gather.sems(3, lines),
+        ],
+        compiler_params=pltpu.CompilerParams(
+            collective_id=ident, has_side_effects=True, vmem_limit_bytes=56 << 20
+        ),
+    )(ids, table, lim, packed, highway)
+
+
+LANE = 128
+TABLE_ROWS = 48
+HEAD_ROWS = 56
+
+
+class Totals:
+    def __init__(self, place, value, inbox, send_sems, recv_sems):
+        self.place, self.value, self.inbox = place, value, inbox
+        self.send_sems, self.recv_sems = send_sems, recv_sems
+        self.partners = [place.sibling, place.across]
+        span = 1
+        while span < place.lines:
+            low = lax.rem(place.line // span, 2)
+            self.partners.append(place.on_line(place.line + span - 2 * span * low))
+            span *= 2
+        self.partners.append(place.partner)
+
+    def start(self, i):
+        self.copy = send(
+            self.value, self.inbox.at[i], (self.send_sems.at[i], self.recv_sems.at[i]), self.partners[i]
+        )
+
+    def end(self, i):
+        self.copy.wait()
+        self.value[...] = self.value[...] + self.inbox[i]
+
+
+def bias_lane(rows, lane, value):
+    return jnp.where(lax.broadcasted_iota(jnp.int32, (rows, LANE), 1) == lane, value, 0.0)
+
+
+def back_kernel(lines, limits, per, pieces, taps_used, *refs):
+    refs = iter(refs)
+
+    def take(n):
+        return [next(refs) for _ in range(n)]
+
+    enc = take(3)
+    (de_ref, base_ref, proj_ref, low_ref, packed_ref, conv_ref, conv_t_ref, lim_ref, ids_ref, vec_in) = take(10)
+    kept_hbm = [take(5), take(5)]
+    pooled_hbm, chars_hbm = take(2)
+    land = take(3 * 7)
+    highway_hbm = take(2)
+    outs = take(7)
+    (vec_ref,) = take(1)
+    scatter_bufs, scatter_sems = take(6), take(7)
+    (kst, knl, kgt, full, wbuf, acc, dpre, dpre_t, gs) = take(9)
+    (demb, leave, come, projg, convg, pack, dchars, chars, inbox) = take(9)
+    (load_s, weight_s, out_s, swap_s, swap_r, total_s, total_r) = take(7)
+
+    place = Place(lines)
+    side = place.side
+    arrays = [*enc, projg, highway_hbm[1], highway_hbm[0], convg]
+    scatter = Scatter(
+        place, arrays, land[:7], land[7:14], land[14:], outs, pieces, scatter_bufs, scatter_sems
+    )
+    of_array = [[k for k, piece in enumerate(pieces) if piece[0] == i] for i in range(7)]
+    main = of_array[6][0]
+    ticks = scatter.order(main)
+    meet(neighbours(place, True))
+
+    def go(kind, k):
+        while (kind, k) in ticks:
+            tick = ticks.pop(0)
+            getattr(scatter, tick[0])(tick[1])
+
+    def begin(i):
+        for k in of_array[i]:
+            scatter.begin(k)
+
+    own, words = gs.shape
+    quarter = own // 4
+    lines_each = lines // 4
+
+    def loads(layer):
+        state, nonlin, gate, both, _ = kept_hbm[layer]
+        copies = [
+            pltpu.make_async_copy(src, dst, load_s.at[i])
+            for i, (src, dst) in enumerate(((state, kst), (nonlin, knl), (gate, kgt), (both, full)))
+        ]
+        for copy in copies:
+            copy.start()
+        return copies
+
+    def weights(layer, q):
+        copy = pltpu.make_async_copy(
+            kept_hbm[layer][4].at[pl.ds(q * lines_each, lines_each)], wbuf.at[q % 2], weight_s.at[q % 2]
+        )
+        copy.start()
+        return copy
+
+    kept_copies = loads(1)
+    weight_copies = [weights(1, 0), weights(1, 1)]
+    de_copy = send(de_ref, demb, (swap_s.at[2], swap_r.at[2]), place.partner)
+    for i in range(3):
+        begin(i)
+    vec_ref[...] = vec_in[...]
+    pack[...] = jnp.zeros_like(pack)
+    go("add_core", 2)
+    de_copy.wait()
+
+    total = jnp.zeros((1, demb.shape[1]), f32)
+    for c in range(words // LANE):
+        rows = pl.ds(c * LANE, LANE)
+        value = (base_ref[rows, :] + demb[rows, :].astype(f32)).astype(bf16)
+        demb[rows, :] = value
+        total = total + jnp.sum(value.astype(f32), axis=0, keepdims=True)
+    total = jnp.where(side == 0, total, 0.0)
+    for j in range(demb.shape[1] // LANE):
+        vec_ref[TABLE_ROWS + j : TABLE_ROWS + j + 1, :] = total[:, j * LANE : (j + 1) * LANE]
+
+    def project(c, carry):
+        rows = pl.ds(pl.multiple_of(c * LANE, LANE), LANE)
+        grad = dot(low_ref[rows, :], demb[...], 1, 0)
+        for j in range(LANE // per):
+            index = c * (LANE // per) + j
+            projg[index // 4, (index // 2) % 2, index % 2, :per, :] = grad[j * per : (j + 1) * per].astype(bf16)
+        gs[rows, :] = dot(proj_ref[rows, :], demb[...], 1, 1)
+        return carry
+
+    lax.fori_loop(0, own // LANE, project, 0)
+    begin(3)
+    go("add_row", 0)
+
+    def layer(l, marks):
+        for copy in kept_copies:
+            copy.wait()
+
+        def slopes(c, carry):
+            rows = pl.ds(pl.multiple_of(c * 64, 64), 64)
+            grad, nonlin, gate = gs[rows, :], knl[rows, :], kgt[rows, :]
+            through = grad * (1.0 - gate)
+            value, slope = gelu_both(nonlin)
+            d_nonlin = through * slope
+            d_gate = grad * (kst[rows, :] - value) * gate * (1.0 - gate)
+            gs[rows, :] = grad * gate
+            both = jnp.stack(
+                [d_nonlin.reshape(64 // per, per, words), d_gate.reshape(64 // per, per, words)], axis=1
+            ).reshape(128, words)
+            dpre[pl.ds(pl.multiple_of(c * 128, 128), 128), :] = both.astype(bf16)
+            dpre_t[:, pl.ds(pl.multiple_of(c * 128, 128), 128)] = both.T.astype(bf16)
+            at = taps_used + 1 + 2 * l
+            pack[rows, :] += bias_lane(64, at, jnp.sum(d_nonlin, axis=1, keepdims=True)) + bias_lane(
+                64, at + 1, jnp.sum(d_gate, axis=1, keepdims=True)
+            )
+            return carry
+
+        lax.fori_loop(0, own // 64, slopes, 0)
+        for q in range(4):
+            weight_copies[q % 2].wait()
+
+            def back(n, carry, q=q):
+                lanes = pl.ds(pl.multiple_of(n * 256, 256), 256)
+                matrix = wbuf[q % 2, :, :, :, :, lanes].reshape(2 * quarter, 256)
+                part = dot(dpre_t[:, 2 * quarter * q : 2 * quarter * (q + 1)], matrix, 1, 0)
+                if q:
+                    part = acc[:, lanes] + part
+                acc[:, lanes] = part
                 return carry
 
-            lax.fori_loop(0, some, convolve, 0)
-
-            def pool(g, carry):
-                here = pl.ds(pl.multiple_of(g * 8, 8), 8)
-                there = pl.ds(pl.multiple_of(block * FBLOCK + g * 8, 8), 8)
-                lim = lim_ref[there, :] if some > full else None
-
-                def entry(p):
-                    value = conv_ref[p, here, :]
-                    return value if p < full else jnp.where(lim[:, :1] >= p, value, big_negative)
-
-                top = entry(0)
-                for p in range(1, some):
-                    top = jnp.maximum(top, entry(p))
-                total = jnp.exp(entry(0) - top)
-                for p in range(1, some):
-                    total = total + jnp.exp(entry(p) - top)
-                pooled_ref[there, lanes] = top + jnp.log(total)
+            lax.fori_loop(0, FILTERS // 256, back, 0)
+            if q < 2:
+                weight_copies[q % 2] = weights(l, q + 2)
+            if marks[q]:
+                go(*marks[q])
+
+        def turn(c, carry):
+            part = acc[:, pl.ds(pl.multiple_of(c * 128, 128), 128)].T.reshape(64 // per, 2, per, words)
+            first, second = part[:, 0].reshape(64, words), part[:, 1].reshape(64, words)
+            rows = pl.ds(pl.multiple_of(c * 64, 64), 64)
+            gs[rows, :] += jnp.where(side == 0, first, second)
+            leave[rows, :] = jnp.where(side == 0, second, first).astype(bf16)
+            return carry
+
+        lax.fori_loop(0, own // 64, turn, 0)
+        swap = send(leave, come.at[l], (swap_s.at[l], swap_r.at[l]), place.partner)
+        stores = [None, None]
+        for q in range(4):
+            if stores[q % 2] is not None:
+                stores[q % 2].wait()
+
+            def grads(n, carry, q=q):
+                lanes = pl.ds(pl.multiple_of(n * 256, 256), 256)
+                part = dot(dpre[2 * quarter * q : 2 * quarter * (q + 1), :], full[lanes, :], 1, 1)
+                wbuf[q % 2, :, :, :, :, lanes] = part.astype(bf16).reshape(
+                    lines_each, 2, 2, 2 * per, 256
+                )
                 return carry
 
-            lax.fori_loop(0, FBLOCK // 8, pool, 0)
-
-
-def conv_forward(ids, table, weight, lim, per):
-    rows = weight.shape[0]
-    words = ids.shape[1]
-    limits = tuple(block_limits(per, s, s + FBLOCK) for s in range(0, rows, FBLOCK))
-    return pl.pallas_call(
-        functools.partial(conv_forward_kernel, limits),
-        out_shape=(
-            jax.ShapeDtypeStruct((rows, words), f32),
-            jax.ShapeDtypeStruct((VROWS, words), bf16),
+            lax.fori_loop(0, FILTERS // 256, grads, 0)
+            stores[q % 2] = pltpu.make_async_copy(
+                wbuf.at[q % 2], highway_hbm[l].at[pl.ds(q * lines_each, lines_each)], out_s.at[q % 2]
+            )
+            stores[q % 2].start()
+            if marks[4 + q]:
+                go(*marks[4 + q])
+        for store in stores:
+            store.wait()
+        return swap
+
+    def arrive(l, swap):
+        swap.wait()
+
+        def add(c, carry):
+            rows = pl.ds(pl.multiple_of(c * 64, 64), 64)
+            gs[rows, :] += come[l, rows, :].astype(f32)
+            return carry
+
+        lax.fori_loop(0, own // 64, add, 0)
+
+    first_hw = [of_array[4][0], of_array[5][0]]
+    swap = layer(1, [None, ("add_core", first_hw[0] - 1), None, ("add_row", 1)] + [None] * 4)
+    kept_copies = loads(0)
+    weight_copies = [weights(0, 0), weights(0, 1)]
+    begin(4)
+    go("add_core", first_hw[1] - 1)
+    arrive(1, swap)
+    swap = layer(0, [None] * 8)
+    begin(5)
+    copies = [
+        pltpu.make_async_copy(pooled_hbm, kst, load_s.at[0]),
+        pltpu.make_async_copy(chars_hbm, chars, load_s.at[3]),
+    ]
+    for copy in copies:
+        copy.start()
+    go("add_core", first_hw[1] + 1)
+    arrive(0, swap)
+    for copy in copies:
+        copy.wait()
+
+    def pooled_grad(c, carry):
+        rows = pl.ds(pl.multiple_of(c * 64, 64), 64)
+        _, slope = gelu_both(kst[rows, :] + packed_ref[rows, taps_used : taps_used + 1])
+        grad = gs[rows, :] * slope
+        gs[rows, :] = grad
+        pack[rows, :] += bias_lane(64, taps_used, jnp.sum(grad, axis=1, keepdims=True))
+        return carry
+
+    lax.fori_loop(0, own // 64, pooled_grad, 0)
+    dchars[...] = jnp.zeros_like(dchars)
+    wgrad = knl.at[:, :TAPS]
+    wgrad[...] = jnp.zeros((own, TAPS), f32)
+    slots = [dpre.at[:own], dpre.at[own:], full.at[:own], full.at[own:]]
+
+    def place_at(p, blocks, slot):
+        window = pl.ds(p * CHAR_DIM if isinstance(p, int) else pl.multiple_of(p * CHAR_DIM, CHAR_DIM), TAPS)
+        taps = chars[window, :]
+        dconv = slots[slot]
+        for block in range(blocks):
+            full_places, _ = limits[block]
+            rows = pl.ds(block * FBLOCK, FBLOCK)
+            value = jnp.exp(dot(conv_ref[rows, :], taps, 1, 0) - kst[rows, :]) * gs[rows, :]
+            if isinstance(p, int) and p >= full_places:
+                value = jnp.where(lim_ref[rows, :][:, :1] >= p, value, 0.0)
+            dconv[rows, :] = value.astype(bf16)
+        rows = pl.ds(0, blocks * FBLOCK)
+        wgrad[rows, :] += dot(dconv[rows, :], taps, 1, 1)
+        dchars[window, :] += dot(conv_t_ref[:, : blocks * FBLOCK], dconv[rows, :], 1, 0)
+
+    always = min(full_places for full_places, _ in limits)
+    ever = max(some for _, some in limits)
+    stretches = 11
+    runs = -(-(always // 4) // stretches)
+    left = len(ticks)
+    done = 0
+    for s in range(stretches):
+        start, stop = s * runs, min((s + 1) * runs, always // 4)
+
+        def four(i, carry):
+            for u in range(4):
+                place_at(i * 4 + u, len(limits), u)
+            return carry
+
+        lax.fori_loop(start, stop, four, 0)
+        while done < left * (s + 1) // (stretches + 2):
+            getattr(scatter, ticks[0][0])(ticks[0][1])
+            ticks.pop(0)
+            done += 1
+    for p in range(always // 4 * 4, ever):
+        blocks = 1 + max(block for block, (_, some) in enumerate(limits) if p < some)
+        place_at(p, blocks, p % 4)
+    lane = lax.broadcasted_iota(jnp.int32, (own, TAPS), 1)
+    keep = (lane < (CHARS - lim_ref[...]) * CHAR_DIM) & (lane < taps_used)
+    result = (pack[...] + jnp.where(keep, wgrad[...], 0.0)).astype(bf16)
+    convg[:, :, :, :per, :] = result.reshape(lines, 2, 2, per, LANE)
+    begin(6)
+
+    ids_count = TABLE_ROWS // CHAR_DIM * LANE
+
+    def spread(c, total):
+        for i in range(5):
+            rows = pl.ds(pl.multiple_of((c * 5 + i) * CHAR_DIM, CHAR_DIM), CHAR_DIM)
+            row = pl.ds(c * 5 + i, 1)
+            ids = jnp.concatenate([ids_ref[0, row, :], ids_ref[1, row, :]], axis=1)
+            total = total + dot(dchars[rows, :].astype(bf16), onehot_chars(ids, ids_count), 1, 1)
+        return total
+
+    table = lax.fori_loop(0, CHARS // 5, spread, jnp.zeros((CHAR_DIM, ids_count), f32))
+    for j in range(ids_count // LANE):
+        vec_ref[j * CHAR_DIM : (j + 1) * CHAR_DIM, :] = table[:, j * LANE : (j + 1) * LANE]
+    totals = Totals(place, vec_ref, inbox, total_s, total_r)
+    while ticks:
+        getattr(scatter, ticks[0][0])(ticks[0][1])
+        ticks.pop(0)
+    last = of_array[6]
+    phases = [scatter.add_core, scatter.add_row, scatter.add_line]
+    for i in range(len(totals.partners)):
+        totals.start(i)
+        if i < 3:
+            for k in last:
+                phases[i](k)
+        totals.end(i)
+    scatter.finish()
+
+
+def embedder_backward(
+    enc, de_low, base, proj_all, low, packed, conv, lim, ids, vec, kept, pooled, chars, lines, per,
+    taps_used, ident,
+):
+    own, words = low.shape
+    limits = tuple(block_limits(per, s, s + FBLOCK) for s in range(0, own, FBLOCK))
+    shape = jax.ShapeDtypeStruct
+    tall = max(per, 16)
+    whole = []
+    for a in enc:
+        rows = -(-a.shape[1] // 16) * 16
+        a = jnp.pad(a, ((0, 0), (0, rows - a.shape[1]), (0, 0)))
+        whole.append(a.reshape((lines, 2, 2) + a.shape[1:]))
+    lead = (lines, 2, 2)
+    width = proj_all.shape[1]
+    made = [
+        shape(lead + (tall, width), bf16),
+        shape(lead + (2 * per, FILTERS), bf16),
+        shape(lead + (2 * per, FILTERS), bf16),
+        shape(lead + (tall, LANE), bf16),
+    ]
+    arrays = whole + made
+    pieces = cut(arrays, 48)
+    land, outs, bufs, sems = Scatter.shapes(arrays, pieces, lines)
+    dma = pltpu.SemaphoreType.DMA
+    vmem = pl.BlockSpec(memory_space=pltpu.VMEM)
+    steps = 3 + (lines - 1).bit_length()
+    layers = [
+        (state, nonlin, gate, both, weight.reshape(lead + (2 * per, FILTERS)))
+        for state, nonlin, gate, both, weight in kept
+    ]
+    result = pl.pallas_call(
+        functools.partial(back_kernel, lines, limits, per, pieces, taps_used),
+        out_shape=tuple(land + [made[1], made[1]] + outs + [shape(vec.shape, f32)]),
+        in_specs=[ANYWHERE] * 4 + [vmem] * 9 + [ANYWHERE] * 12,
+        out_specs=tuple([ANYWHERE] * (len(land) + 2) + [vmem] * (len(outs) + 1)),
+        scratch_shapes=bufs
+        + sems
+        + [
+            pltpu.VMEM((own, words), f32), pltpu.VMEM((own, words), f32), pltpu.VMEM((own, words), f32),
+            pltpu.VMEM((2 * own, words), bf16),
+            pltpu.VMEM((2, lines // 4, 2, 2, 2 * per, FILTERS), bf16),
+            pltpu.VMEM((words, FILTERS), f32),
+            pltpu.VMEM((2 * own, words), bf16), pltpu.VMEM((words, 2 * own), bf16),
+            pltpu.VMEM((own, words), f32), pltpu.VMEM((words, width), bf16),
+            pltpu.VMEM((own, words), bf16),
+            pltpu.VMEM((2, own, words), bf16),
+            pltpu.VMEM(made[0].shape, bf16), pltpu.VMEM(made[3].shape, bf16),
+            pltpu.VMEM((own, LANE), f32), pltpu.VMEM((VROWS, words), f32), pltpu.VMEM((VROWS, words), bf16),
+            pltpu.VMEM((steps,) + vec.shape, f32),
+            dma((4,)), dma((2,)), dma((2,)), dma((3,)), dma((3,)), dma((steps,)), dma((steps,)),
+        ],
+        compiler_params=pltpu.CompilerParams(
+            collective_id=ident, has_side_effects=True, vmem_limit_bytes=62 << 20
         ),
-        scratch_shapes=[pltpu.VMEM((CHARS, FBLOCK, FBLOCK), f32)],
-        compiler_params=pltpu.CompilerParams(vmem_limit_bytes=48 << 20),
-        cost_estimate=pl.CostEstimate(flops=14 * 10**9, bytes_accessed=8 << 20, transcendentals=24 * 10**6),
-    )(ids, table, weight, lim)
-
-
-def conv_backward_kernel(
-    limits, ids_ref, chars_ref, weight_ref, weight_t_ref, lim_ref, pooled_ref, grad_ref,
-    weight_grad_ref, table_grad_ref, dconv_ref, dchars_ref,
-):
-    words = ids_ref.shape[1]
-    count = table_grad_ref.shape[1]
-    dchars_ref[...] = jnp.zeros_like(dchars_ref)
-    weight_grad_ref[...] = jnp.zeros_like(weight_grad_ref)
-    table_grad_ref[...] = jnp.zeros_like(table_grad_ref)
-    always = min(full for full, some in limits)
-    ever = max(some for full, some in limits)
-
-    def place(p, blocks):
-        if isinstance(p, int):
-            window = pl.ds(p * CHAR_DIM, TAPS)
-        else:
-            window = pl.ds(pl.multiple_of(p * CHAR_DIM, CHAR_DIM), TAPS)
-        for block in blocks:
-            full, some = limits[block]
-            rows = pl.ds(block * FBLOCK, FBLOCK)
-            taps = chars_ref[window, :]
-            weights = jnp.exp(dot(weight_ref[rows, :], taps, 1, 0) - pooled_ref[rows, :])
-            value = weights * grad_ref[rows, :]
-            if isinstance(p, int) and p >= full:
-                value = jnp.where(lim_ref[rows, :][:, :1] >= p, value, 0.0)
-            value = value.astype(bf16)
-            dconv_ref[rows, :] = value
-            weight_grad_ref[rows, :] += dot(value, taps, 1, 1)
-        count_rows = len(blocks) * FBLOCK
-        dchars_ref[window, :] += dot(weight_t_ref[:, :count_rows], dconv_ref[:count_rows, :], 1, 0)
-
-    everyone = range(len(limits))
-
-    def step(p, carry):
-        place(p, everyone)
-        return carry
-
-    lax.fori_loop(0, always, step, 0)
-    for p in range(always, ever):
-        blocks = [block for block, (full, some) in enumerate(limits) if p < some]
-        place(p, range(max(blocks) + 1))
-
-    def spread(c, carry):
-        rows = pl.ds(pl.multiple_of(c * CHAR_DIM, CHAR_DIM), CHAR_DIM)
-        hot = onehot_chars(ids_ref[pl.ds(c, 1), :], count)
-        table_grad_ref[...] += dot(dchars_ref[rows, :].astype(bf16), hot, 1, 1)
-        return carry
-
-    lax.fori_loop(0, CHARS, spread, 0)
-
-
-def conv_backward(ids, chars, weight, lim, pooled, grad, per, count):
-    rows = weight.shape[0]
-    words = ids.shape[1]
-    limits = tuple(block_limits(per, s, s + FBLOCK) for s in range(0, rows, FBLOCK))
-    return pl.pallas_call(
-        functools.partial(conv_backward_kernel, limits),
-        out_shape=(
-            jax.ShapeDtypeStruct((rows, TAPS), f32),
-            jax.ShapeDtypeStruct((CHAR_DIM, count), f32),
-        ),
-        scratch_shapes=[pltpu.VMEM((rows, words), bf16), pltpu.VMEM((VROWS, words), f32)],
-        compiler_params=pltpu.CompilerParams(vmem_limit_bytes=48 << 20),
-        cost_estimate=pl.CostEstimate(flops=42 * 10**9, bytes_accessed=8 << 20, transcendentals=24 * 10**6),
-    )(ids, chars, weight, weight.T, lim, pooled, grad)
+    )(
+        *whole, de_low, base, proj_all, low, packed, conv, conv.T, lim, ids, vec,
+        *layers[0], *layers[1], pooled, chars,
+    )
+    outs = result[len(land) + 2 : -1]
+    heights = [a.shape[1] for a in enc] + [per, 2 * per, 2 * per, per]
+    return [o[:h] for o, h in zip(outs, heights)], result[-1]
 
 
 def norm_forward(summed):
@@ -706,21 +1040,17 @@
     lines = ndp // 4
     blocks = [highway_t[i].reshape(2 * per, FILTERS) for i in range(layers)]
     highway_all = [None] * layers
-    packed_all, highway_all[0] = gather_blocks([packed, blocks[0]], lines, 1)
-    packed_all = packed_all.reshape(own, TAPS)
-    highway_all[0] = highway_all[0].reshape(2 * own, FILTERS)
 
     filter_index = jnp.arange(own, dtype=jnp.int32)
     filter_index = (filter_index // per) * (2 * per) + side * per + filter_index % per
     filter_width = width_of(filter_index).astype(jnp.int32)
     lim = jnp.broadcast_to((CHARS - filter_width)[:, None], (own, 128))
-    tap_shift = jnp.arange(TAPS, dtype=jnp.int32) // CHAR_DIM
-    conv_all = jnp.where(
-        (tap_shift[None, :] < filter_width[:, None]) & (jnp.arange(TAPS) < taps_used)[None, :],
-        packed_all,
-        0.0,
-    ).astype(bf16)
-    conv_bias_all = packed_all[:, taps_used][:, None]
+    table_t = jnp.pad(char_table.T, ((0, 0), (0, padded_ids - ids_count)))
+    (
+        packed_all, highway_all[0], ids, chars, conv_all, pooled_raw, state, state_low, other_low,
+    ) = embed_words(char_ids.T, table_t, lim, packed, blocks[0], lines, per, 1)
+    packed_all = packed_all.reshape(own, TAPS)
+    highway_all[0] = highway_all[0].reshape(2 * own, FILTERS)
 
     def layer_bias(i):
         both = packed_all[:, taps_used + 1 + 2 * i : taps_used + 3 + 2 * i]
@@ -733,27 +1063,20 @@
         second = jnp.where(side == 0, theirs, mine)
         return jnp.concatenate([first, second], axis=1).reshape(FILTERS, words)
 
-    ids = lax.all_gather(char_ids.T, PAIR, axis=1, tiled=True)
-    table_t = jnp.pad(char_table.T, ((0, 0), (0, padded_ids - ids_count)))
-    pooled_raw, chars = conv_forward(ids, table_t, conv_all, lim, per)
-    pooled = pooled_raw + conv_bias_all
-    state = gelu(pooled)
     kept = []
     for i in range(layers):
-        state_low = state.astype(bf16)
         if i == 0:
-            *highways, proj_all, other_low = gather_blocks(
-                blocks[1:] + [proj_weight], lines, 2, state_low
-            )
+            *highways, proj_all = gather_blocks(blocks[1:] + [proj_weight], lines, 2)
             highway_all[1:] = [h.reshape(2 * own, FILTERS) for h in highways]
             proj_all = proj_all.reshape(own, D)
         else:
+            state_low = state.astype(bf16)
             other_low = pair_swap(state_low)
         state_full = both_sides(state_low, other_low)
         pre = dot(highway_all[i], state_full, 1, 0).reshape(ndp, 2, per, words) + layer_bias(i)
         nonlin = pre[:, 0].reshape(own, words)
         gate = jax.nn.sigmoid(pre[:, 1].reshape(own, words))
-        kept.append((state, state_full, nonlin, gate))
+        kept.append((state, nonlin, gate, state_full, highway_all[i]))
         state = gate * state + (1.0 - gate) * gelu(nonlin)
     state_low = state.astype(bf16)
     emb_part = dot(state_low, proj_all, 0, 0)
@@ -831,7 +1154,7 @@
     dffn = grad_second.astype(bf16)
     down_bias_grad = jnp.sum(dffn, axis=0, dtype=f32)
     down_grad_t = dot(dffn, hidden_s, 0, 0)
-    dpre = (dot(dffn, down_weight, 1, 1) * gelu_slope(hidden_pre_s)).astype(bf16)
+    dpre = (dot(dffn, down_weight, 1, 1) * gelu_both(hidden_pre_s)[1]).astype(bf16)
     up_bias_grad = jnp.sum(dpre, axis=0, dtype=f32)
     up_grad = dot(normed_low_s, dpre, 0, 0)
     dn_part = dot(dpre, up_weight, 1, 1)
@@ -864,79 +1187,31 @@
         g.astype(bf16).reshape(ndp, D // ndp, -1)
         for g in (up_grad, down_grad_t, jnp.concatenate(qkvo_grad, axis=1))
     ]
-    up_mine, down_mine, qkvo_mine, de_other = scatter_blocks(
-        encoder_grads, lines, 3, swap=de_part.astype(bf16)
-    )
-    grad_embedded = back[:, D:] + (de_part + de_other.astype(f32))
-    demb = grad_embedded.astype(bf16)
-
-    proj_bias_grad = jnp.sum(demb, axis=0, dtype=f32)
-    proj_grad = dot(state_low, demb, 1, 0)
-    grad_state = dot(proj_all, demb, 1, 1)
-    highway_mine = [None] * layers
-    highway_bias_grads = [None] * layers
-    for i in reversed(range(layers)):
-        state_in, state_full, nonlin, gate = kept[i]
-        d_nonlin = (grad_state * (1.0 - gate) * gelu_slope(nonlin)).astype(bf16)
-        d_gate = (grad_state * (state_in - gelu(nonlin)) * gate * (1.0 - gate)).astype(bf16)
-        d_pre = jnp.stack(
-            [d_nonlin.reshape(ndp, per, words), d_gate.reshape(ndp, per, words)], axis=1
-        ).reshape(2 * own, words)
-        highway_grad = dot(d_pre, state_full, 1, 1).astype(bf16).reshape(ndp, 2 * per, FILTERS)
-        highway_bias_grads[i] = jnp.sum(d_pre, axis=1, dtype=f32)
-        back_part = dot(highway_all[i], d_pre, 0, 0).reshape(ndp, 2, per, words)
-        mine = jnp.where(side == 0, back_part[:, 0], back_part[:, 1]).reshape(own, words)
-        other = jnp.where(side == 0, back_part[:, 1], back_part[:, 0]).reshape(own, words)
-        ready = [highway_grad]
-        if i == layers - 1:
-            ready.append(proj_grad.astype(bf16).reshape(ndp, per, D))
-        highway_mine[i], *rest, theirs = scatter_blocks(ready, lines, 4 + i, swap=other.astype(bf16))
-        if rest:
-            proj_mine = rest[0]
-        grad_state = grad_state * gate + (mine + theirs.astype(f32))
-    grad_pooled = grad_state * gelu_slope(pooled)
-    conv_bias_grad = jnp.sum(grad_pooled, axis=1)
-    conv_grad, table_grad_t = conv_backward(
-        ids, chars, conv_all, lim, pooled_raw, grad_pooled, per, padded_ids
-    )
-    tap_mask = (tap_shift[None, :] < filter_width[:, None])[:, :taps_used]
-    conv_grad = jnp.where(tap_mask, conv_grad[:, :taps_used], 0.0)
-
-    bias_grads = [conv_bias_grad[:, None]]
-    for i in range(layers):
-        both = highway_bias_grads[i].reshape(ndp, 2, per).transpose(0, 2, 1).reshape(own, 2)
-        bias_grads.append(both)
-    conv_pack = jnp.concatenate(
-        [conv_grad, *bias_grads, jnp.zeros((own, TAPS - taps_used - 1 - 2 * layers), f32)], axis=1
-    )
-    (conv_mine,) = scatter_blocks([conv_pack.reshape(ndp, per, TAPS)], lines, 4 + layers)
     first = side == 0
     shared = [
         jnp.where(first, g, 0.0)
         for g in (
-            proj_bias_grad, out_bias_grad, ln1_gain_grad, ln1_bias_grad, down_bias_grad,
-            ln2_gain_grad, ln2_bias_grad,
+            out_bias_grad, ln1_gain_grad, ln1_bias_grad, down_bias_grad, ln2_gain_grad, ln2_bias_grad,
         )
     ]
     own_side = jnp.concatenate([qv_bias_grad.reshape(-1), up_bias_grad])
-    flat = jnp.concatenate(
-        [
-            table_grad_t.reshape(-1),
-            *shared,
-            jnp.where(first, own_side, 0.0),
-            jnp.where(first, 0.0, own_side),
-        ]
-    )
+    flat = jnp.concatenate([*shared, jnp.where(first, own_side, 0.0), jnp.where(first, 0.0, own_side)])
     rows_flat = -(-flat.shape[0] // 1024) * 8
-    flat = jnp.pad(flat, (0, rows_flat * 128 - flat.shape[0])).reshape(rows_flat, 128)
-    flat = total_all(flat, lines, 5 + layers).reshape(-1)
-    at = table_grad_t.size
-    table_grad_t = flat[:at].reshape(table_grad_t.shape)
-    (
-        proj_bias_grad, out_bias_grad, ln1_gain_grad, ln1_bias_grad, down_bias_grad, ln2_gain_grad,
-        ln2_bias_grad,
-    ) = (flat[at + i * D : at + (i + 1) * D] for i in range(7))
-    at += 7 * D
+    flat = jnp.pad(flat, (HEAD_ROWS * LANE, rows_flat * LANE - flat.shape[0])).reshape(-1, LANE)
+
+    (up_mine, down_mine, qkvo_mine, proj_mine, *highway_mine, conv_mine), flat = embedder_backward(
+        encoder_grads, de_part.astype(bf16), back[:, D:] + de_part, proj_all, state_low, packed_all,
+        conv_all, lim, ids, flat, kept, pooled_raw, chars, lines, per, taps_used, 3,
+    )
+    highway_mine = highway_mine[::-1]
+    table_grad_t = flat[:TABLE_ROWS].reshape(-1, CHAR_DIM, LANE).transpose(1, 0, 2).reshape(CHAR_DIM, -1)
+    flat = flat[TABLE_ROWS:].reshape(-1)
+    proj_bias_grad = flat[:D]
+    flat = flat[(HEAD_ROWS - TABLE_ROWS) * LANE :]
+    out_bias_grad, ln1_gain_grad, ln1_bias_grad, down_bias_grad, ln2_gain_grad, ln2_bias_grad = (
+        flat[i * D : (i + 1) * D] for i in range(6)
+    )
+    at = 6 * D
     size = own_side.shape[0]
     own_side = jnp.where(first, flat[at : at + size], flat[at + size : at + 2 * size])
     qv_bias_grad = own_side[: 2 * width].reshape(2, width)

time: 839 us -> 554 us (0.66)
  Pallas kernels: 534 us -> 372 us
  matrix products: 105 us -> 60.8 us
  local copies, waits for them, and re-layouts: 65.1 us -> 36.6 us
  other arithmetic: 56.9 us -> 28.8 us
  waiting for transfers between devices: 51.3 us -> 39.7 us
    pallas_call x7 -> x2, Pallas kernels: 418 us -> 311 us  [the longest x1 231 us: embedder_backward(): pl.pallas_call(functools.partial(back_kernel, lines, limits, per, pieces,...]
    pallas_call x2 -> x1, Pallas kernels: 117 us -> 61 us  [gather_blocks(): pl.pallas_call(functools.partial(gather_kernel, lines, count, len(swaps))...]
    dot_general x34 -> x28, matrix products: 85.5 us -> 45.3 us  [dot(): lax.dot_general(a, b, (((ca,), (cb,)), ((), ())), preferred_element_type=...]
    dot_general x3 -> x1, local copies, waits for them, and re-layouts: 26.3 us -> 1.41 us  [dot(): lax.dot_general(a, b, (((ca,), (cb,)), ((), ())), preferred_element_type=...]
    convert_element_type x3 -> x2, other arithmetic: 18 us -> 2.78 us  [per_device(): state_low = state.astype(bf16)]
    ppermute x5, waiting for transfers between devices: 51.3 us -> 39.7 us  [pair_swap(): return lax.ppermute(x, PAIR, [(0, 1), (1, 0)])]
  transfers between devices with their start and end apart: 5 -> 5, of which waited for: 4 -> 4; matrix products, arithmetic and copies ran while one was open for 5% -> 3% of each run, Pallas kernels for 0% -> 11%
where the time goes in v2:
time: 554 us; the launch traced here: 543 us
  Pallas kernels  372 us (67%)
  matrix products  60.8 us (11%)
  waiting for transfers between devices  39.7 us (7%)
  local copies, waits for them, and re-layouts  36.6 us (7%)
  other arithmetic  28.8 us (5%)
    pallas_call x1, Pallas kernels, embedder_backward(): pl.pallas_call(functools.partial(back_kernel, lines, limits, per, pieces,...  231 us
    pallas_call x1, Pallas kernels, embed_words(): pl.pallas_call(functools.partial(embed_kernel, lines, limits), out_shape=...  79.7 us
    pallas_call x1, Pallas kernels, gather_blocks(): pl.pallas_call(functools.partial(gather_kernel, lines, count, len(swaps))...  61 us
    dot_general x28, matrix products, dot(): lax.dot_general(a, b, (((ca,), (cb,)), ((), ())), preferred_element_type=...  45.3 us
    ppermute x5, waiting for transfers between devices, pair_swap(): return lax.ppermute(x, PAIR, [(0, 1), (1, 0)])  39.7 us
    unnamed x149, local copies, waits for them, and re-layouts  13.9 us
  transfers between devices with their start and end apart: 5, of which 4 were waited for; matrix products, arithmetic and copies ran while one was open for 3% of the time, Pallas kernels for 11%

profile of v2, /device:TPU:0, one launch (start us, length us, event | category | flops | bytes accessed | tf_op | source)
XLA Modules:
  0.0 542.8 jit_solution(8291216045544175205)
XLA Ops:
  3.0 2.3 fusion.95
  7.7 79.7 %shard_map.366 = (f32[4,2,2,64,128]{4,3,2,1,0:T(8,128)}, bf16[4,2,2,128,2048]{4,3,2,1,0:T(8,128)(2,1)}, s32[2,50,256]{2,1,0:T(8,128)}, bf16[912,512]{1,0:T(8,128...) custom-call(s32[50,256]{1,0:T(8,128)} %bitcast.277, ...), custom_call_target="tpu_custom_call" | custom-call | tf_op jit(solution)/shard_map/pallas_call | solution.py:589
  87.4 1.7 broadcast_select_fusion.3
  92.7 6.9 %broadcast_add_fusion.1 = f32[16,2,64,512]{3,2,1,0:T(8,128)S(1)} fusion(f32[16,2,64]{2,1,0:T(2,128)S(1)} %copy.64, bf16[16,2,64,2048]{3,2,1,0:T(8,128)(2,1)} %bitcast.228, bf16[2048,512,1,1]{1,0,3,2:T(8,128)(2,1)S(1)} %bitcast.224), kind=kOutput, calls=%fused_computation.31 | convolution fusion | flops 4296015872 | bytes 14688256 | tf_op jit(solution)/shard_map/dot_general | solution.py:45
  101.2 1.9 fusion.94
  103.8 61.0 %shard_map.365 = (bf16[4,2,2,128,2048]{4,3,2,1,0:T(8,128)(2,1)}, bf16[4,2,2,64,768]{4,3,2,1,0:T(8,128)(2,1)}) custom-call(bf16[128,2048]{1,0:T(8,128)(2,1)} %bitcast.244, bf16[64,768]{1,0:T(8,128)(2,1)} %refs_1_.1), custom_call_target="tpu_custom_call" | custom-call | tf_op jit(solution)/shard_map/pallas_call | solution.py:244
  164.9 1.8 broadcast_select_fusion.1
  169.6 4.5 broadcast_add_fusion
  179.4 18.9 %collective-permute-done.1 = bf16[512,768]{1,0:T(8,128)(2,1)S(1)} collective-permute-done((bf16[512,768]{1,0:T(8,128)(2,1)S(1)}, bf16[512,768]{1,0:T(8,128)(2,1)S(1)}, u32[]{:S(2)}, u32[]{:S(2)}) %collective-permute-start.1) | collective-permute-done | bytes 786464 | tf_op jit(solution)/shard_map/ppermute | solution.py:62
  200.2 4.8 fusion.99
  205.0 3.5 fusion.21
  209.3 1.8 fusion.100
  215.8 2.3 fusion.103
  218.1 11.9 %collective-permute-done.2 = bf16[512,768]{1,0:T(8,128)(2,1)} collective-permute-done((bf16[512,768]{1,0:T(8,128)(2,1)S(1)}, bf16[512,768]{1,0:T(8,128)(2,1)}, u32[]{:S(2)}, u32[]{:S(2)}) %collective-permute-start.2) | collective-permute-done | bytes 786464 | tf_op jit(solution)/shard_map/ppermute | solution.py:62
  229.9 2.8 fusion.93
  236.3 6.8 %fusion.31 = f32[512,768]{1,0:T(8,128)} fusion(bf16[1536,768]{1,0:T(8,128)(2,1)} %param.40, bf16[768,1536]{1,0:T(8,128)(2,1)} %param.38, f32[1536]{0:T(1024)} %convert_element_type.314, f32[512,768]{1,0:T(8,128)} %copy-done.6), kind=kOutput, calls=%fused_computation.84 | convolution fusion | flops 2421030912 | bytes 7870464 | tf_op jit(solution)/shard_map/dot_general | solution.py:45
  243.1 2.9 fusion.101
  249.5 1.7 copy.69
  254.8 5.6 %collective-permute-done.3 = bf16[336,768]{1,0:T(8,128)(2,1)} collective-permute-done((bf16[336,768]{1,0:T(8,128)(2,1)}, bf16[336,768]{1,0:T(8,128)(2,1)}, u32[]{:S(2)}, u32[]{:S(2)}) %collective-permute-start.3) | collective-permute-done | bytes 516128 | tf_op jit(solution)/shard_map/ppermute | solution.py:62
  264.7 2.3 convolution_convert_fusion
  267.9 2.2 convolution_convert_fusion.1
  272.2 3.4 collective-permute-done.4
  276.4 1.4 convolution_convert_fusion.2
  278.0 2.6 convert_reduce_fusion
  283.6 1.5 subtract_convert_fusion.2
  286.1 1.6 convolution_convert_fusion.4
  290.6 2.0 slice_add_fusion
  292.6 1.7 pad_maximum_fusion.refs_2_
  294.2 231.2 %shard_map.367 = (bf16[4,2,48,1536]{3,2,1,0:T(8,128)(2,1)}, bf16[4,2,48,1536]{3,2,1,0:T(8,128)(2,1)}, bf16[4,2,48,1536]{3,2,1,0:T(8,128)(2,1)}, bf16[4,2,64,768]...) custom-call(bf16[4,2,2,48,1536]{4,3,2,1,0:T(8,128)(2,1)} %bitcast.22, ...), custom_call_target="tpu_custom_call" | custom-call | tf_op jit(solution)/shard_map/pallas_call | solution.py:961
  529.0 1.5 slice_reduce_fusion
  534.1 1.7 slice_bitcast_fusion.9
  535.8 3.2 maximum_bitcast_fusion
  (264 shorter events, 61.8 us)
Async XLA Ops:
  0.7 208.6 %copy-start = (bf16[384,768]{1,0:T(8,128)(2,1)S(1)}, bf16[384,768]{1,0:T(8,128)(2,1)}, u32[]{:S(2)}) copy-start(bf16[384,768]{1,0:T(8,128)(2,1)} %param.34) | copy-start | bytes 1769476
  0.7 4.7 copy-start.58
  89.5 10.1 %copy-start.11 = (bf16[16,2,64,512]{3,2,1,0:T(8,128)(2,1)}, bf16[16,2,64,512]{3,2,1,0:T(8,128)(2,1)S(1)}, u32[]{:S(2)}) copy-start(bf16[16,2,64,512]{3,2,1,0:T(8,128)(2,1)S(1)} %copy.63) | copy-start | bytes 6291460
  103.1 71.8 %copy-start.1 = (f32[1024,512]{1,0:T(8,128)}, f32[1024,512]{1,0:T(8,128)S(1)}, u32[]{:S(2)}) copy-start(f32[1024,512]{1,0:T(8,128)S(1)} %get-tuple-element.83.refs_18_) | copy-start | bytes 6291460
  103.1 61.8 %collective-permute-start = (bf16[1024,512]{1,0:T(8,128)(2,1)}, bf16[1024,512]{1,0:T(8,128)(2,1)}, u32[]{:S(2)}, u32[]{:S(2)}) collective-permute-start(bf16[1024,512]{1,0:T(8,128)(2,1)} %get-tuple-element.82), channel_id=1, source_target_pairs={{0,1},{1,0},{2,3},{3,2},{4,5},{5,4},{6,7},{7,6},{8,9},{9,8},{10,11... | collective-permute-start | bytes 3145736 | tf_op jit(solution)/shard_map/ppermute | solution.py:62
  164.9 4.8 copy-start.14
  178.5 20.4 %copy-start.16 = (f32[512,768]{1,0:T(8,128)}, f32[512,768]{1,0:T(8,128)S(1)}, u32[]{:S(2)}) copy-start(f32[512,768]{1,0:T(8,128)S(1)} %get-tuple-element.114) | copy-start | bytes 4718596
  178.5 19.9 %copy-start.23 = (bf16[768,3,384]{2,0,1:T(8,128)(2,1)S(1)}, bf16[768,3,384]{2,0,1:T(8,128)(2,1)}, u32[]{:S(2)}) copy-start(bf16[768,3,384]{2,0,1:T(8,128)(2,1)} %param.32) | copy-start | bytes 5308420
  178.6 19.7 %collective-permute-start.1 = (bf16[512,768]{1,0:T(8,128)(2,1)S(1)}, bf16[512,768]{1,0:T(8,128)(2,1)S(1)}, u32[]{:S(2)}, u32[]{:S(2)}) collective-permute-start(bf16[512,768]{1,0:T(8,128)(2,1)S(1)} %get-tuple-element.113), channel_id=1, source_target_pairs={{0,1},{1,0},{2,3},{3,2},{4,5},{5,4},{6,7},{7,6},{8,9},{9,8},{10,11... | collective-permute-start | bytes 2359304 | tf_op jit(solution)/shard_map/ppermute | solution.py:62
  198.4 50.2 %copy-start.15 = (bf16[512,768]{1,0:T(8,128)(2,1)}, bf16[512,768]{1,0:T(8,128)(2,1)S(1)}, u32[]{:S(2)}) copy-start(bf16[512,768]{1,0:T(8,128)(2,1)S(1)} %fusion.25) | copy-start | bytes 2359300
  199.1 16.6 %copy-start.29 = (bf16[512,384]{0,1:T(8,128)(2,1)}, bf16[512,384]{0,1:T(8,128)(2,1)S(1)}, u32[]{:S(2)}) copy-start(bf16[512,384]{0,1:T(8,128)(2,1)S(1)} %fusion.19) | copy-start | bytes 1179652
  199.7 5.4 copy-start.71
  200.2 4.8 copy-start.69
  208.6 4.3 copy-start.39
  208.6 5.0 copy-start.33
  209.3 5.2 copy-start.68
  211.0 18.9 %collective-permute-start.2 = (bf16[512,768]{1,0:T(8,128)(2,1)S(1)}, bf16[512,768]{1,0:T(8,128)(2,1)}, u32[]{:S(2)}, u32[]{:S(2)}) collective-permute-start(bf16[512,768]{1,0:T(8,128)(2,1)S(1)} %get-tuple-element.117), channel_id=1, source_target_pairs={{0,1},{1,0},{2,3},{3,2},{4,5},{5,4},{6,7},{7,6},{8,9},{9,8},{10,11... | collective-permute-start | bytes 2359304 | tf_op jit(solution)/shard_map/ppermute | solution.py:62
  211.6 49.9 %copy-start.41 = (f32[768]{0:T(1024)}, f32[768]{0:T(1024)S(1)}, u32[]{:S(2)}) copy-start(f32[768]{0:T(1024)S(1)} %convert_element_type.319) | copy-start | bytes 9220
  214.4 19.0 %copy-start.49 = (s32[80]{0:T(128)}, s32[80]{0:T(128)S(1)}, u32[]{:S(2)}) copy-start(s32[80]{0:T(128)S(1)} %pad.17) | copy-start | bytes 964
  243.1 5.5 %copy-start.50 = (s32[80]{0:T(128)S(1)}, s32[80]{0:T(128)}, u32[]{:S(2)}) copy-start(s32[80]{0:T(128)} %copy-done.49) | copy-start | bytes 964
  248.0 12.4 %collective-permute-start.3 = (bf16[336,768]{1,0:T(8,128)(2,1)}, bf16[336,768]{1,0:T(8,128)(2,1)}, u32[]{:S(2)}, u32[]{:S(2)}) collective-permute-start(bf16[336,768]{1,0:T(8,128)(2,1)} %pad_maximum_fusion.3), channel_id=1, source_target_pairs={{0,1},{1,0},{2,3},{3,2},{4,5},{5,4},{6,7},{7,6},{8,9},{9,8},{10,11... | collective-permute-start | bytes 1548296 | tf_op jit(solution)/shard_map/ppermute | solution.py:62
  252.7 8.9 %copy-start.34 = (f32[80,768]{1,0:T(8,128)S(1)}, f32[80,768]{1,0:T(8,128)}, u32[]{:S(2)}) copy-start(f32[80,768]{1,0:T(8,128)} %get-tuple-element.120) | copy-start | bytes 737284
  252.7 8.9 %copy-start.45 = (f32[512]{0:T(512)S(1)}, f32[512]{0:T(512)}, u32[]{:S(2)}) copy-start(f32[512]{0:T(512)} %copy-done.44) | copy-start | bytes 6148
  252.7 8.9 %copy-start.48 = (f32[512]{0:T(512)S(1)}, f32[512]{0:T(512)}, u32[]{:S(2)}) copy-start(f32[512]{0:T(512)} %copy-done.47) | copy-start | bytes 6148
  252.7 8.9 %copy-start.51 = (s32[80]{0:T(128)S(1)}, s32[80]{0:T(128)}, u32[]{:S(2)}) copy-start(s32[80]{0:T(128)} %copy-done.49) | copy-start | bytes 964
  254.8 7.5 %copy-start.22 = (f32[1,76,768]{2,1,0:T(8,128)S(1)}, f32[1,76,768]{2,1,0:T(8,128)}, u32[]{:S(2)}) copy-start(f32[1,76,768]{2,1,0:T(8,128)} %copy.92) | copy-start | bytes 700420
  270.6 5.8 %copy-start.28 = (bf16[6,64,512]{2,1,0:T(8,128)(2,1)S(1)}, bf16[6,64,512]{2,1,0:T(8,128)(2,1)}, u32[]{:S(2)}) copy-start(bf16[6,64,512]{2,1,0:T(8,128)(2,1)} %copy-done.27) | copy-start | bytes 1179652
  270.6 5.8 %copy-start.52 = (s32[80]{0:T(128)S(1)}, s32[80]{0:T(128)}, u32[]{:S(2)}) copy-start(s32[80]{0:T(128)} %copy-done.49) | copy-start | bytes 964
  270.7 4.9 collective-permute-start.4
  535.8 4.4 copy-start.40
  535.8 5.1 copy-start.38
  535.8 5.8 %copy-start.37 = (f32[48,1536]{1,0:T(8,128)S(1)}, f32[48,1536]{1,0:T(8,128)}, u32[]{:S(2)}) copy-start(f32[48,1536]{1,0:T(8,128)} %get-tuple-element.57) | copy-start | bytes 884740
  (45 other events, 91.0 us)
